TPU v7x, 32 devices: a whole 2x2x4 slice. The times are simulated.
32 devices in a mesh: dp: 16 (over z, y, x), tensor: 2 (over core).
Axes of the slice: x: 2, y: 2, z: 4, core: 2. Of those that a mesh axis runs over, the one named last changes fastest.
Arguments:
- content_input: bfloat16 [16384, 768], P('dp'), may hold values from -6 to 6
- query_input: bfloat16 [16384, 768], P('dp'), may hold values from -6 to 6
- segment_ids: int32 [32, 512], P('dp'), may hold values from 0 to 15, never falling along the last dimension, each value on 1 to 256 neighbouring positions
- orders: int32 [32, 512], P('dp'), may hold values from 0 to 511, each once within a row
- predicted: int32 [32, 512], P('dp'), may hold values 0 or 1
- query_weight: bfloat16 [768, 768], P(None, 'tensor'), may hold values from -0.21875 to 0.21875
- query_bias: float32 [768], P('tensor'), may hold values from -3 to 3
- key_weight: bfloat16 [768, 768], P(None, 'tensor'), may hold values from -0.21875 to 0.21875
- value_weight: bfloat16 [768, 768], P(None, 'tensor'), may hold values from -0.21875 to 0.21875
- value_bias: float32 [768], P('tensor'), may hold values from -3 to 3
- out_weight: bfloat16 [768, 768], P('tensor'), may hold values from -0.875 to 0.875
- out_bias: float32 [768], replicated, may hold values from -3 to 3
- first_gain: float32 [768], replicated, may hold values from 0.25 to 1.75
- first_shift: float32 [768], replicated, may hold values from -2 to 2
- up_weight: bfloat16 [768, 3072], P(None, 'tensor'), may hold values from -0.21875 to 0.21875
- up_bias: float32 [3072], P('tensor'), may hold values from -3 to 3
- down_weight: bfloat16 [3072, 768], P('tensor'), may hold values from -0.109375 to 0.109375
- down_bias: float32 [768], replicated, may hold values from -3 to 3
- second_gain: float32 [768], replicated, may hold values from 0.25 to 1.75
- second_shift: float32 [768], replicated, may hold values from -2 to 2
- bias_table: float32 [32, 12], P(None, 'tensor'), may hold values from -4 to 4
- content_upstream: bfloat16 [16384, 768], P(('dp', 'tensor')), may hold values from -6 to 6
- query_upstream: bfloat16 [16384, 768], P(('dp', 'tensor')), may hold values from -6 to 6
Outputs:
- content_out: bfloat16 [16384, 768], P(('dp', 'tensor'))
- query_out: bfloat16 [16384, 768], P(('dp', 'tensor'))
- grad_content: float32 [16384, 768], P(('dp', 'tensor'))
- grad_query: float32 [16384, 768], P(('dp', 'tensor'))
- grad_query_weight: float32 [768, 768], P('dp', 'tensor')
- grad_key_weight: float32 [768, 768], P('dp', 'tensor')
- grad_value_weight: float32 [768, 768], P('dp', 'tensor')
- grad_out_weight: float32 [768, 768], P('tensor', 'dp')
- grad_up_weight: float32 [768, 3072], P('dp', 'tensor')
- grad_down_weight: float32 [3072, 768], P('tensor', 'dp')
- grad_query_bias: float32 [768], replicated
- grad_value_bias: float32 [768], replicated
- grad_out_bias: float32 [768], replicated
- grad_first_gain: float32 [768], replicated
- grad_first_shift: float32 [768], replicated
- grad_up_bias: float32 [3072], replicated
- grad_down_bias: float32 [768], replicated
- grad_second_gain: float32 [768], replicated
- grad_second_shift: float32 [768], replicated
- grad_bias_table: float32 [32, 12], replicated
Inputs may be any that keep to these rules, and one draw needn't show every extreme that they name: `segment_ids`: along each row the segment numbers never fall; a segment covers 1 to 256 positions. `orders`: each row holds every number once.
All inputs are finite; a program needn't handle non-finite values. No bound on the sum of `predicted` on one device may be relied on, other than what follows from the above.
Results may differ from a plain program's by a relative error of at most 0.015.
Values may be sent and summed in bfloat16 or wider, within the bound.
No kernel may reach another device: no remote copies, remote signals or barrier semaphores. Data moves between devices by JAX's collectives and lax.ppermute only.
A program may use at most 192 MiB of HBM per device.

v0:
```python
import jax
import jax.numpy as jnp
import numpy as np
from jax import lax
from jax.sharding import PartitionSpec as P

norm_eps = 1e-05
big_negative = -1e30
root_half = 0.7071067811865476
root_two_pi_inv = 0.3989422804014327


def bucket_grid(length):
    offsets = np.arange(length)
    distance = np.abs(offsets[:, None] - offsets[None, :])
    limits = 8.0 * 2.0 ** (np.arange(1, 8) / 2.0)
    counted = (distance[:, :, None] >= limits[None, None, :]).sum(axis=2)
    bucket = np.where(distance < 8, distance, 8 + counted)
    bucket = np.minimum(bucket, 15) + 16 * (offsets[None, :] > offsets[:, None])
    return bucket.astype(np.int32)


def layer_norm(values, gain_vec, shift_vec):
    centre = jnp.mean(values, axis=-1, keepdims=True)
    centred = values - centre
    variance = jnp.mean(centred * centred, axis=-1, keepdims=True)
    inv_scale = lax.rsqrt(variance + norm_eps)
    normed = centred * inv_scale
    return (normed * gain_vec + shift_vec, normed, inv_scale)


def norm_back(upstream, normed, inv_scale, gain_vec):
    scaled = upstream * gain_vec
    centre = jnp.mean(scaled, axis=-1, keepdims=True)
    along_normed = jnp.mean(scaled * normed, axis=-1, keepdims=True)
    return inv_scale * (scaled - centre - normed * along_normed)


def gelu_parts(pre_act):
    normal_cdf = 0.5 * (1.0 + lax.erf(pre_act * root_half))
    slope = normal_cdf + pre_act * jnp.exp(-0.5 * pre_act * pre_act) * root_two_pi_inv
    return (pre_act * normal_cdf, slope)


def row_masks(segment, ordering, flagged):
    same_doc = segment[:, None] == segment[None, :]
    unmasked = (flagged == 0)[None, :]
    earlier = ordering[None, :] < ordering[:, None]
    itself = ordering[None, :] == ordering[:, None]
    starts = jnp.concatenate([jnp.ones((1,), dtype=bool), segment[1:] != segment[:-1]])
    content_mask = same_doc & (unmasked | earlier | itself)
    query_mask = same_doc & (unmasked | earlier | starts[None, :])
    return jnp.stack([content_mask, query_mask])


def row_scores(queries, keys_low, pos_bias, visible, score_scale):
    raw_scores = jnp.einsum("sqhd,khd->shqk", queries, keys_low, preferred_element_type=jnp.float32)
    scores = raw_scores * score_scale + pos_bias[None]
    return jnp.where(visible[:, None], scores, big_negative)


def place_block(part_vec, whole_len, block_index):
    zeros_full = jnp.zeros((whole_len,) + part_vec.shape[1:], jnp.float32)
    return lax.dynamic_update_slice_in_dim(zeros_full, part_vec, block_index * part_vec.shape[0], 0)


def local(
    content_input,
    query_input,
    segment_ids,
    orders,
    predicted,
    query_weight,
    query_bias,
    key_weight,
    value_weight,
    value_bias,
    out_weight,
    out_bias,
    first_gain,
    first_shift,
    up_weight,
    up_bias,
    down_weight,
    down_bias,
    second_gain,
    second_shift,
    bias_table,
    content_upstream,
    query_upstream,
):
    tensor_count = lax.axis_size("tensor")
    tensor_index = lax.axis_index("tensor")
    tok_count = content_input.shape[0]
    row_count = segment_ids.shape[0]
    row_len = segment_ids.shape[1]
    model_width = query_weight.shape[0]
    local_heads = bias_table.shape[1]
    local_width = query_weight.shape[1]
    head_size = local_width // local_heads
    score_scale = head_size ** (-0.5)
    half_rows = tok_count // tensor_count
    own_start = tensor_index * half_rows
    streams = jnp.stack([content_input, query_input])
    queries_low = (
        jnp.einsum("stn,nm->stm", streams, query_weight, preferred_element_type=jnp.float32)
        + query_bias
    ).astype(jnp.bfloat16)
    keys_low = jnp.dot(content_input, key_weight, preferred_element_type=jnp.float32).astype(
        jnp.bfloat16
    )
    values_low = (
        jnp.dot(content_input, value_weight, preferred_element_type=jnp.float32) + value_bias
    ).astype(jnp.bfloat16)
    bucket_ids = jnp.asarray(bucket_grid(row_len)).reshape(-1)
    one_hot = (
        bucket_ids[:, None] == jnp.arange(bias_table.shape[0], dtype=jnp.int32)[None, :]
    ).astype(jnp.float32)
    pos_bias = jnp.einsum(
        "pb,bh->hp", one_hot, bias_table, precision=lax.Precision.HIGHEST
    ).reshape(local_heads, row_len, row_len)

    def row_inputs(row_index):
        row_start = row_index * row_len
        row_query = lax.dynamic_slice_in_dim(queries_low, row_start, row_len, 1).reshape(
            2, row_len, local_heads, head_size
        )
        row_key = lax.dynamic_slice_in_dim(keys_low, row_start, row_len, 0).reshape(
            row_len, local_heads, head_size
        )
        row_value = lax.dynamic_slice_in_dim(values_low, row_start, row_len, 0).reshape(
            row_len, local_heads, head_size
        )
        visible = row_masks(segment_ids[row_index], orders[row_index], predicted[row_index])
        scores = row_scores(row_query, row_key, pos_bias, visible, score_scale)
        return (row_start, row_query, row_key, row_value, scores)

    def attend_row(mixed_all, row_index):
        row_start, row_query, row_key, row_value, scores = row_inputs(row_index)
        row_top = jnp.max(scores, axis=-1, keepdims=True)
        log_total = row_top + jnp.log(jnp.sum(jnp.exp(scores - row_top), axis=-1, keepdims=True))
        weights = jnp.exp(scores - log_total).astype(jnp.bfloat16)
        mixed_out = jnp.einsum(
            "shqk,khd->sqhd", weights, row_value, preferred_element_type=jnp.float32
        )
        mixed_out = mixed_out.astype(jnp.bfloat16).reshape(2, row_len, local_width)
        return (lax.dynamic_update_slice_in_dim(mixed_all, mixed_out, row_start, 1), log_total)

    attn_low, log_totals = lax.scan(
        attend_row, jnp.zeros((2, tok_count, local_width), jnp.bfloat16), jnp.arange(row_count)
    )
    attn_part = jnp.einsum("stm,mn->stn", attn_low, out_weight, preferred_element_type=jnp.float32)
    attn_rows = lax.psum_scatter(attn_part, "tensor", scatter_dimension=1, tiled=True)
    own_streams = lax.dynamic_slice_in_dim(streams, own_start, half_rows, 1).astype(jnp.float32)
    own_first, first_normed, first_inv = layer_norm(
        own_streams + attn_rows + out_bias, first_gain, first_shift
    )
    first_out = lax.all_gather(own_first.astype(jnp.bfloat16), "tensor", axis=1, tiled=True).astype(
        own_first.dtype
    )
    first_low = first_out.astype(jnp.bfloat16)
    up_pre = (
        jnp.einsum("stn,nf->stf", first_low, up_weight, preferred_element_type=jnp.float32)
        + up_bias
    )
    hidden, slope = gelu_parts(up_pre)
    hidden_low = hidden.astype(jnp.bfloat16)
    down_part = jnp.einsum(
        "stf,fn->stn", hidden_low, down_weight, preferred_element_type=jnp.float32
    )
    down_own = lax.psum_scatter(
        down_part.astype(jnp.bfloat16), "tensor", scatter_dimension=1, tiled=True
    ).astype(jnp.float32)
    final_out, second_normed, second_inv = layer_norm(
        own_first + down_own + down_bias, second_gain, second_shift
    )
    upstream = jnp.stack([content_upstream, query_upstream]).astype(jnp.float32)
    second_own = norm_back(upstream, second_normed, second_inv, second_gain)
    gain_two_grad = jnp.sum(upstream * second_normed, axis=(0, 1))
    shift_two_grad = jnp.sum(upstream, axis=(0, 1))
    down_bias_grad = jnp.sum(second_own, axis=(0, 1))
    second_grad = lax.all_gather(
        second_own.astype(jnp.bfloat16), "tensor", axis=1, tiled=True
    ).astype(second_own.dtype)
    down_low = second_grad.astype(jnp.bfloat16)
    down_weight_grad = jnp.einsum(
        "stf,stn->fn", hidden_low, down_low, preferred_element_type=jnp.float32
    )
    hidden_grad = jnp.einsum(
        "stn,fn->stf", down_low, down_weight, preferred_element_type=jnp.float32
    )
    up_low = (hidden_grad * slope).astype(jnp.bfloat16)
    up_bias_grad = jnp.sum(up_low.astype(jnp.float32), axis=(0, 1))
    up_weight_grad = jnp.einsum(
        "stn,stf->nf", first_low, up_low, preferred_element_type=jnp.float32
    )
    first_part = jnp.einsum("stf,nf->stn", up_low, up_weight, preferred_element_type=jnp.float32)
    back_own = (
        lax.psum_scatter(
            first_part.astype(jnp.bfloat16), "tensor", scatter_dimension=1, tiled=True
        ).astype(jnp.float32)
        + second_own
    )
    residual_own = norm_back(back_own, first_normed, first_inv, first_gain)
    first_pre_grad = lax.all_gather(
        residual_own.astype(jnp.bfloat16), "tensor", axis=1, tiled=True
    ).astype(residual_own.dtype)
    gain_one_grad = jnp.sum(back_own * first_normed, axis=(0, 1))
    shift_one_grad = jnp.sum(back_own, axis=(0, 1))
    out_bias_grad = jnp.sum(residual_own, axis=(0, 1))
    attn_grad_low = first_pre_grad.astype(jnp.bfloat16)
    out_weight_grad = jnp.einsum(
        "stm,stn->mn", attn_low, attn_grad_low, preferred_element_type=jnp.float32
    )
    mixed_grad = jnp.einsum(
        "stn,mn->stm", attn_grad_low, out_weight, preferred_element_type=jnp.float32
    ).astype(jnp.bfloat16)

    def back_row(buffers, row_index):
        query_grads, key_grads, value_grads, bias_grad = buffers
        row_start, row_query, row_key, row_value, scores = row_inputs(row_index)
        row_mixed = lax.dynamic_slice_in_dim(mixed_grad, row_start, row_len, 1).reshape(
            2, row_len, local_heads, head_size
        )
        row_probs = jnp.exp(scores - log_totals[row_index])
        prob_grad = jnp.einsum(
            "sqhd,khd->shqk", row_mixed, row_value, preferred_element_type=jnp.float32
        )
        row_delta = jnp.sum(row_probs * prob_grad, axis=-1, keepdims=True)
        score_grad = (row_probs * (prob_grad - row_delta)).astype(jnp.bfloat16)
        query_piece = (
            jnp.einsum("shqk,khd->sqhd", score_grad, row_key, preferred_element_type=jnp.float32)
            * score_scale
        ).astype(jnp.bfloat16)
        key_piece = (
            jnp.einsum("shqk,sqhd->khd", score_grad, row_query, preferred_element_type=jnp.float32)
            * score_scale
        ).astype(jnp.bfloat16)
        value_piece = jnp.einsum(
            "shqk,sqhd->khd",
            row_probs.astype(jnp.bfloat16),
            row_mixed,
            preferred_element_type=jnp.float32,
        ).astype(jnp.bfloat16)
        query_grads = lax.dynamic_update_slice_in_dim(
            query_grads, query_piece.reshape(2, row_len, local_width), row_start, 1
        )
        key_grads = lax.dynamic_update_slice_in_dim(
            key_grads, key_piece.reshape(row_len, local_width), row_start, 0
        )
        value_grads = lax.dynamic_update_slice_in_dim(
            value_grads, value_piece.reshape(row_len, local_width), row_start, 0
        )
        bias_grad = bias_grad + jnp.sum(score_grad.astype(jnp.float32), axis=0)
        return ((query_grads, key_grads, value_grads, bias_grad), None)

    start_buffers = (
        jnp.zeros((2, tok_count, local_width), jnp.bfloat16),
        jnp.zeros((tok_count, local_width), jnp.bfloat16),
        jnp.zeros((tok_count, local_width), jnp.bfloat16),
        jnp.zeros((local_heads, row_len, row_len), jnp.float32),
    )
    (query_grads, key_grads, value_grads, bias_grad), unused_rows = lax.scan(
        back_row, start_buffers, jnp.arange(row_count)
    )
    query_weight_grad = jnp.einsum(
        "stn,stm->nm", streams, query_grads, preferred_element_type=jnp.float32
    )
    key_weight_grad = jnp.einsum(
        "tn,tm->nm", content_input, key_grads, preferred_element_type=jnp.float32
    )
    value_weight_grad = jnp.einsum(
        "tn,tm->nm", content_input, value_grads, preferred_element_type=jnp.float32
    )
    query_bias_grad = jnp.sum(query_grads.astype(jnp.float32), axis=(0, 1))
    value_bias_grad = jnp.sum(value_grads.astype(jnp.float32), axis=0)
    table_grad = jnp.einsum(
        "pb,hp->hb",
        one_hot,
        bias_grad.reshape(local_heads, row_len * row_len),
        precision=lax.Precision.HIGHEST,
    )
    content_extra = jnp.einsum(
        "tm,nm->tn", key_grads, key_weight, preferred_element_type=jnp.float32
    ) + jnp.einsum("tm,nm->tn", value_grads, value_weight, preferred_element_type=jnp.float32)
    input_part = jnp.einsum(
        "stm,nm->stn", query_grads, query_weight, preferred_element_type=jnp.float32
    )
    input_part = jnp.stack([input_part[0] + content_extra, input_part[1]])
    input_own = (
        lax.psum_scatter(
            input_part.astype(jnp.bfloat16), "tensor", scatter_dimension=1, tiled=True
        ).astype(jnp.float32)
        + residual_own
    )
    (
        query_weight_grad,
        key_weight_grad,
        value_weight_grad,
        out_weight_grad,
        up_weight_grad,
        down_weight_grad,
    ) = (
        lax.psum_scatter(query_weight_grad, "dp", scatter_dimension=0, tiled=True),
        lax.psum_scatter(key_weight_grad, "dp", scatter_dimension=0, tiled=True),
        lax.psum_scatter(value_weight_grad, "dp", scatter_dimension=0, tiled=True),
        lax.psum_scatter(out_weight_grad, "dp", scatter_dimension=1, tiled=True),
        lax.psum_scatter(up_weight_grad, "dp", scatter_dimension=0, tiled=True),
        lax.psum_scatter(down_weight_grad, "dp", scatter_dimension=1, tiled=True),
    )
    summed = lax.psum(
        (
            gain_one_grad,
            shift_one_grad,
            out_bias_grad,
            gain_two_grad,
            shift_two_grad,
            down_bias_grad,
            place_block(query_bias_grad, model_width, tensor_index),
            place_block(value_bias_grad, model_width, tensor_index),
            place_block(up_bias_grad, up_bias.shape[0] * tensor_count, tensor_index),
            place_block(table_grad, local_heads * tensor_count, tensor_index),
        ),
        ("dp", "tensor"),
    )
    return (
        final_out[0].astype(jnp.bfloat16),
        final_out[1].astype(jnp.bfloat16),
        input_own[0],
        input_own[1],
        query_weight_grad,
        key_weight_grad,
        value_weight_grad,
        out_weight_grad,
        up_weight_grad,
        down_weight_grad,
        summed[6],
        summed[7],
        summed[2],
        summed[0],
        summed[1],
        summed[8],
        summed[5],
        summed[3],
        summed[4],
        summed[9].T,
    )


def solution(mesh):
    placed = (
        P("dp", None),
        P("dp", None),
        P("dp", None),
        P("dp", None),
        P("dp", None),
        P(None, "tensor"),
        P("tensor"),
        P(None, "tensor"),
        P(None, "tensor"),
        P("tensor"),
        P("tensor", None),
        P(),
        P(),
        P(),
        P(None, "tensor"),
        P("tensor"),
        P("tensor", None),
        P(),
        P(),
        P(),
        P(None, "tensor"),
        P(("dp", "tensor"), None),
        P(("dp", "tensor"), None),
    )
    return jax.shard_map(
        local,
        mesh=mesh,
        in_specs=placed,
        out_specs=(
            P(("dp", "tensor"), None),
            P(("dp", "tensor"), None),
            P(("dp", "tensor"), None),
            P(("dp", "tensor"), None),
            P("dp", "tensor"),
            P("dp", "tensor"),
            P("dp", "tensor"),
            P("tensor", "dp"),
            P("dp", "tensor"),
            P("tensor", "dp"),
            P(),
            P(),
            P(),
            P(),
            P(),
            P(),
            P(),
            P(),
            P(),
            P(),
        ),
        check_vma=False,
    )
```

profile of v0, /device:TPU:0, one launch (start us, length us, event | category | flops | bytes accessed | tf_op | source)
XLA Modules:
  0.0 1269.4 jit_solution(3649579443299737185)
XLA Ops:
  14.9 5.0 add_convert_fusion.1
  22.5 12.1 convolution_bitcast_fusion
  36.0 94.2 %while.29 = (s32[]{:T(128)}, bf16[2,1024,384]{1,2,0:T(8,128)(2,1)}, f32[2,2,6,512,1]{3,1,2,4,0:T(2,128)S(1)}, s32[2]{0:T(128)S(1)}, bf16[1024,384]{0,1:T(8,128)(...) while((s32[]{:T(128)}, bf16[2,1024,384]{1,2,0:T(8,128)(2,1)}, ...), condition=%wide.region_3.4_spmd, body=%wide.region_0.3_spmd.sunk | while | flops 852356608 | bytes 139417056 | solution.py:149
  43.3 9.7 copy.243
  53.0 6.6 copy.244
  59.6 8.2 fusion.148
  67.9 6.7 exponential_reduce_fusion.2
  74.6 7.2 fusion.149
  90.4 9.7 copy.243
  100.0 6.6 copy.244
  106.6 8.2 fusion.148
  114.9 6.7 exponential_reduce_fusion.2
  121.7 7.2 fusion.149
  130.2 6.0 fusion.77
  136.7 16.9 %reduce-scatter.15.cloned.1.call-done = f32[2,512,768]{2,1,0:T(8,128)} async-done(((f32[2,1024,768]{2,1,0:T(8,128)}), f32[2,512,768]{2,1,0:T(8,128)}) %reduce-scatter.15.cloned.1.call-update) | async-done | bytes 3145744 | tf_op jit(solution)/shard_map/reduce_scatter | solution.py:153
  160.0 13.4 %all-gather.4.cloned.1.call-done = bf16[2,1024,768]{2,1,0:T(8,128)(2,1)} async-done(((bf16[2,512,768]{2,1,0:T(8,128)(2,1)}), bf16[2,1024,768]{2,1,0:T(8,128)(2,1)}) %all-gather.4.cloned.1.call-update) | async-done | bytes 3145744 | tf_op jit(solution)/shard_map/all_gather | solution.py:158
  173.4 9.5 multiply_convert_fusion.1
  185.5 6.4 fusion.68
  192.0 12.2 reduce-scatter.17.cloned.1.call-done
  214.6 13.4 %all-gather.6.cloned.1.call-done = bf16[2,1024,768]{2,1,0:T(8,128)(2,1)} async-done(((bf16[2,512,768]{2,1,0:T(8,128)(2,1)}), bf16[2,1024,768]{2,1,0:T(8,128)(2,1)}) %all-gather.6.cloned.1.call-update) | async-done | bytes 3145744 | tf_op jit(solution)/shard_map/all_gather | solution.py:182
  228.0 12.4 convert_reduce_fusion.1
  243.0 6.4 fusion.65
  249.5 12.2 reduce-scatter.19.cloned.1.call-done
  272.2 13.4 %all-gather.8.cloned.1.call-done = bf16[2,1024,768]{2,1,0:T(8,128)(2,1)} async-done(((bf16[2,512,768]{2,1,0:T(8,128)(2,1)}), bf16[2,1024,768]{2,1,0:T(8,128)(2,1)}) %all-gather.8.cloned.1.call-update) | async-done | bytes 3145744 | tf_op jit(solution)/shard_map/all_gather | solution.py:205
  293.8 149.9 %while.30 = (s32[]{:T(128)}, bf16[2,1024,384]{1,2,0:T(8,128)(2,1)}, bf16[1024,384]{0,1:T(8,128)(2,1)}, bf16[1024,384]{0,1:T(8,128)(2,1)}, f32[6,512,512]{1,2,0:T...) while((s32[]{:T(128)}, bf16[2,1024,384]{1,2,0:T(8,128)(2,1)}, ...), condition=%wide.region_18.19_spmd.clone, body=%wide.region_15.18_spmd.clone.sunk | while | flops 2056580608 | bytes 289683200 | solution.py:263
  302.0 9.7 copy.251
  311.7 6.6 copy.252
  320.1 9.7 fusion.160
  329.8 20.3 %convert_reduce_fusion.6 = (f32[6,512,512]{1,2,0:T(8,128)}, bf16[2,6,512,512]{2,3,0,1:T(8,128)(2,1)}, bf16[2,6,512,512]{2,3,0,1:T(8,128)(2,1)}) fusion(f32[2,6,512,512]{2,3,0,1:T(8,128)} %get-tuple-element.740, f32[2,6,512]{2,0,1:T(2,128)S(1)} %get-tuple-element.741, f32[6,512,2,512]{3,1,2,0:T(8,128)S(1)} %fusion.159), kind=kLoop, calls=%fused_computation.40.clone.1 | loop fusion | flops 17301504 | bytes 44064768 | tf_op jit(solution)/shard_map/while/body/eval_jaxpr/reduce_sum | solution.py:254
  355.1 4.9 fusion.162
  376.7 9.7 copy.251
  386.4 6.6 copy.252
  394.8 9.7 fusion.160
  404.5 20.3 %convert_reduce_fusion.6 = (f32[6,512,512]{1,2,0:T(8,128)}, bf16[2,6,512,512]{2,3,0,1:T(8,128)(2,1)}, bf16[2,6,512,512]{2,3,0,1:T(8,128)(2,1)}) fusion(f32[2,6,512,512]{2,3,0,1:T(8,128)} %get-tuple-element.740, f32[2,6,512]{2,0,1:T(2,128)S(1)} %get-tuple-element.741, f32[6,512,2,512]{3,1,2,0:T(8,128)S(1)} %fusion.159), kind=kLoop, calls=%fused_computation.40.clone.1 | loop fusion | flops 17301504 | bytes 44064768 | tf_op jit(solution)/shard_map/while/body/eval_jaxpr/reduce_sum | solution.py:254
  429.8 4.9 fusion.162
  452.3 10.0 convolution_bitcast_fusion.1
  462.4 10.0 convolution_bitcast_fusion.2
  472.5 5.3 convolution_bitcast_fusion.3
  495.6 6.7 copy.173
  502.3 10.0 copy.201
  513.3 18.5 %fusion.39 = f32[6,32]{1,0:T(8,128)S(1)} fusion(f32[6,262144]{1,0:T(8,128)} %bitcast.302, s32[262144]{0:T(1024)S(1)} %copy-done.28), kind=kOutput, calls=%fused_computation.78 | convolution fusion | flops 612368384 | bytes 7340800 | tf_op jit(solution)/shard_map/pb,hp->hb/dot_general | solution.py:277
  532.0 42.1 %all-reduce = (f32[768]{0:T(1024)}, f32[768]{0:T(1024)}, f32[768]{0:T(1024)}, f32[768]{0:T(1024)}, f32[768]{0:T(1024)}, /*index=5*/f32[3072]{0:T(1024)}, f32[768...) all-reduce(f32[768]{0:T(1024)S(1)} %dynamic_update_slice.28, ...), channel_id=1, replica_groups=mesh['dp'=16,'tensor'=2] {'dp','tensor'}, use_global_device_ids=true, to_apply=%region_27.28 | all-reduce | flops 9600 | bytes 76800 | tf_op jit(solution)/shard_map/psum | solution.py:311
  578.8 29.9 %reduce-scatter.29.cloned.1.call-done = f32[1536,48]{0,1:T(8,128)} async-done(((f32[1536,768]{0,1:T(8,128)}), f32[1536,48]{0,1:T(8,128)}) %reduce-scatter.29.cloned.1.call-update) | async-done | bytes 294928 | tf_op jit(solution)/shard_map/reduce_scatter | solution.py:309
  608.8 142.0 %reduce-scatter.27.cloned.1.call-done = f32[48,1536]{1,0:T(8,128)} async-done(((f32[768,1536]{1,0:T(8,128)}), f32[48,1536]{1,0:T(8,128)}) %reduce-scatter.27.cloned.1.call-update) | async-done | bytes 294928 | tf_op jit(solution)/shard_map/reduce_scatter | solution.py:308
  750.8 127.9 %reduce-scatter.25.cloned.1.call-done = f32[384,48]{0,1:T(8,128)} async-done(((f32[384,768]{0,1:T(8,128)}), f32[384,48]{0,1:T(8,128)}) %reduce-scatter.25.cloned.1.call-update) | async-done | bytes 73744 | tf_op jit(solution)/shard_map/reduce_scatter | solution.py:307
  878.8 128.0 %reduce-scatter.31.cloned.1.call-done = f32[48,384]{1,0:T(8,128)} async-done(((f32[768,384]{1,0:T(8,128)}), f32[48,384]{1,0:T(8,128)}) %reduce-scatter.31.cloned.1.call-update) | async-done | bytes 73744
  1006.7 127.9 %reduce-scatter.23.cloned.1.call-done = f32[48,384]{1,0:T(8,128)} async-done(((f32[768,384]{1,0:T(8,128)}), f32[48,384]{1,0:T(8,128)}) %reduce-scatter.23.cloned.1.call-update) | async-done | bytes 73744 | tf_op jit(solution)/shard_map/reduce_scatter | solution.py:304
  1134.7 128.0 %reduce-scatter.33.cloned.1.call-done = f32[48,384]{1,0:T(8,128)} async-done(((f32[768,384]{1,0:T(8,128)}), f32[48,384]{1,0:T(8,128)}) %reduce-scatter.33.cloned.1.call-update) | async-done | bytes 73744
  (305 shorter events, 138.0 us)
Async XLA Ops:
  7.2 166.2 %copy-start = (bf16[768,1536]{1,0:T(8,128)(2,1)S(1)}, bf16[768,1536]{1,0:T(8,128)(2,1)}, u32[]{:S(2)}) copy-start(bf16[768,1536]{1,0:T(8,128)(2,1)} %param.42) | copy-start | bytes 7077892
  7.2 146.4 %reduce-scatter.15.cloned.1.call-start = ((), (), s32[]{:S(2)}) async-start(), calls=%async_computation.10 | async-start | bytes 9437184 | tf_op jit(solution)/shard_map/reduce_scatter | solution.py:153
  10.0 4.9 copy-start.51
  22.5 13.5 %copy-start.29 = (s32[2,512]{1,0:T(2,128)S(1)}, s32[2,512]{1,0:T(2,128)}, u32[]{:S(2)}) copy-start(s32[2,512]{1,0:T(2,128)} %param.30) | copy-start | bytes 12292
  22.5 13.5 %copy-start.33 = (s32[2,512]{1,0:T(2,128)S(1)}, s32[2,512]{1,0:T(2,128)}, u32[]{:S(2)}) copy-start(s32[2,512]{1,0:T(2,128)} %param.31) | copy-start | bytes 12292
  22.5 13.5 %copy-start.34 = (s32[2,512]{1,0:T(2,128)S(1)}, s32[2,512]{1,0:T(2,128)}, u32[]{:S(2)}) copy-start(s32[2,512]{1,0:T(2,128)} %param.32) | copy-start | bytes 12292
  59.6 8.2 copy-start.2
  67.8 6.8 copy-start.15
  74.6 7.3 copy-start.19
  106.6 8.2 copy-start.2
  114.9 6.8 copy-start.15
  121.6 7.3 copy-start.19
  136.2 17.4 %copy-start.46 = (f32[768]{0:T(1024)S(1)}, f32[768]{0:T(1024)}, u32[]{:S(2)}) copy-start(f32[768]{0:T(1024)} %param.39) | copy-start | bytes 9220
  136.3 37.1 %all-gather.4.cloned.1.call-start = ((), (), s32[]{:S(2)}) async-start(), calls=%async_computation.11 | async-start | bytes 4718592 | tf_op jit(solution)/shard_map/all_gather | solution.py:158
  158.2 15.2 %copy-start.50 = (f32[1536]{0:T(1024)S(1)}, f32[1536]{0:T(1024)}, u32[]{:S(2)}) copy-start(f32[1536]{0:T(1024)} %param.43) | copy-start | bytes 18436
  159.9 44.3 %reduce-scatter.17.cloned.1.call-start = ((), (), s32[]{:S(2)}) async-start(), calls=%async_computation.12 | async-start | bytes 4718592 | tf_op jit(solution)/shard_map/reduce_scatter | solution.py:171
  173.4 12.2 copy-start.49
  192.0 12.3 copy-start.47
  192.0 36.0 %all-gather.6.cloned.1.call-start = ((), (), s32[]{:S(2)}) async-start(), calls=%async_computation.13 | async-start | bytes 4718592 | tf_op jit(solution)/shard_map/all_gather | solution.py:182
  214.5 47.2 %reduce-scatter.19.cloned.1.call-start = ((), (), s32[]{:S(2)}) async-start(), calls=%async_computation.14 | async-start | bytes 4718592 | tf_op jit(solution)/shard_map/reduce_scatter | solution.py:199
  249.5 36.1 %all-gather.8.cloned.1.call-start = ((), (), s32[]{:S(2)}) async-start(), calls=%async_computation.15 | async-start | bytes 4718592 | tf_op jit(solution)/shard_map/all_gather | solution.py:205
  261.7 4.9 copy-start.6
  261.7 5.2 copy-start.8
  261.7 5.6 copy-start.21
  270.8 14.8 %copy-start.30 = (bf16[384,768]{1,0:T(8,128)(2,1)S(1)}, bf16[384,768]{1,0:T(8,128)(2,1)}, u32[]{:S(2)}) copy-start(bf16[384,768]{1,0:T(8,128)(2,1)} %param.38) | copy-start | bytes 1769476
  272.1 302.0 %reduce-scatter.21.cloned.1.call-start = ((), (), s32[]{:S(2)}) async-start(), calls=%async_computation.16 | async-start | bytes 4718592 | tf_op jit(solution)/shard_map/reduce_scatter | solution.py:291
  350.1 13.2 %slice-start.2 = ((s8[6291456]{0:T(1024)(128)(4,1)}), s8[4194304]{0:T(1024)(128)(4,1)S(1)}, s32[]{:S(2)}) async-start(s8[6291456]{0:T(1024)(128)(4,1)} %bitcast.285), calls=%async_computation.25 | async-start | bytes 8388608 | tf_op jit(solution)/shard_map/while
  355.1 5.0 copy-start.3
  355.1 8.3 slice-start.3
  424.8 13.2 %slice-start.2 = ((s8[6291456]{0:T(1024)(128)(4,1)}), s8[4194304]{0:T(1024)(128)(4,1)S(1)}, s32[]{:S(2)}) async-start(s8[6291456]{0:T(1024)(128)(4,1)} %bitcast.285), calls=%async_computation.25 | async-start | bytes 8388608 | tf_op jit(solution)/shard_map/while
  429.7 5.0 copy-start.3
  429.7 8.3 slice-start.3
  452.3 156.5 %reduce-scatter.29.cloned.1.call-start = ((), (), s32[]{:S(2)}) async-start(), calls=%async_computation.20 | async-start | bytes 5013504 | tf_op jit(solution)/shard_map/reduce_scatter | solution.py:309
  462.4 288.4 %reduce-scatter.27.cloned.1.call-start = ((), (), s32[]{:S(2)}) async-start(), calls=%async_computation.19 | async-start | bytes 5013504 | tf_op jit(solution)/shard_map/reduce_scatter | solution.py:308
  472.5 5.6 copy-start.26
  472.5 406.3 %reduce-scatter.25.cloned.1.call-start = ((), (), s32[]{:S(2)}) async-start(), calls=%async_computation.18 | async-start | bytes 1253376 | tf_op jit(solution)/shard_map/reduce_scatter | solution.py:307
  477.8 528.9 %reduce-scatter.31.cloned.1.call-start = ((), (), s32[]{:S(2)}) async-start(), calls=%async_computation.21 | async-start | bytes 1253376
  484.1 650.5 %reduce-scatter.23.cloned.1.call-start = ((), (), s32[]{:S(2)}) async-start(), calls=%async_computation.17 | async-start | bytes 1253376 | tf_op jit(solution)/shard_map/reduce_scatter | solution.py:304
  488.9 773.7 %reduce-scatter.33.cloned.1.call-start = ((), (), s32[]{:S(2)}) async-start(), calls=%async_computation.22 | async-start | bytes 1253376
  491.2 4.1 copy-start.44
  502.3 11.0 copy-start.28
  513.3 18.7 %copy-start.37 = (f32[768]{0:T(1024)S(1)}, f32[768]{0:T(1024)}, u32[]{:S(2)}) copy-start(f32[768]{0:T(1024)} %get-tuple-element.442) | copy-start | bytes 9220
  513.3 18.7 %copy-start.38 = (f32[768]{0:T(1024)S(1)}, f32[768]{0:T(1024)}, u32[]{:S(2)}) copy-start(f32[768]{0:T(1024)} %get-tuple-element.447) | copy-start | bytes 9220
  513.3 18.7 %copy-start.39 = (f32[768]{0:T(1024)S(1)}, f32[768]{0:T(1024)}, u32[]{:S(2)}) copy-start(f32[768]{0:T(1024)} %get-tuple-element.448) | copy-start | bytes 9220
  513.3 18.7 %copy-start.40 = (f32[768]{0:T(1024)S(1)}, f32[768]{0:T(1024)}, u32[]{:S(2)}) copy-start(f32[768]{0:T(1024)} %get-tuple-element.517) | copy-start | bytes 9220
  513.3 18.7 %copy-start.42 = (f32[768]{0:T(1024)S(1)}, f32[768]{0:T(1024)}, u32[]{:S(2)}) copy-start(f32[768]{0:T(1024)} %get-tuple-element.444) | copy-start | bytes 9220
  513.3 18.7 %copy-start.43 = (f32[768]{0:T(1024)S(1)}, f32[768]{0:T(1024)}, u32[]{:S(2)}) copy-start(f32[768]{0:T(1024)} %get-tuple-element.450) | copy-start | bytes 9220
  574.1 688.5 %copy-start.1 = (bf16[768,1536]{1,0:T(8,128)(2,1)S(1)}, bf16[768,1536]{1,0:T(8,128)(2,1)}, u32[]{:S(2)}) copy-start(bf16[768,1536]{1,0:T(8,128)(2,1)} %param.42) | copy-start | bytes 7077892
  (42 other events, 99.7 us)
Sparse Core Ops, SparseCore 0:
  136.4 17.1 reduce-scatter.14
  160.0 13.2 all-gather.3
  192.1 12.0 reduce-scatter.16
  214.7 13.2 all-gather.5
  249.6 12.0 reduce-scatter.18
  272.2 13.2 all-gather.7
  452.4 12.0 reduce-scatter.20
  470.3 138.4 reduce-scatter.28
  615.3 135.4 reduce-scatter.26
  756.0 122.7 reduce-scatter.24
  884.1 122.5 reduce-scatter.30
  1011.9 122.7 reduce-scatter.22
  1140.0 122.6 reduce-scatter.32
where the time goes:
time: 1280 us; the launch traced here: 1270 us
  waiting for transfers between devices  765 us (60%)
  matrix products  203 us (16%)
  local copies, waits for them, and re-layouts  141 us (11%)
  other arithmetic  90.2 us (7%)
  blocking collectives  42.1 us (3%)
  between operations  14.6 us (1%)
    unnamed x15, waiting for transfers between devices  256 us
    reduce_scatter x1, waiting for transfers between devices, local(): lax.psum_scatter(up_weight_grad, 'dp', scatter_dimension=0, tiled=True)  142 us
    reduce_scatter x1, waiting for transfers between devices, local(): lax.psum_scatter(query_weight_grad, 'dp', scatter_dimension=0, tiled=True)  128 us
    reduce_scatter x1, waiting for transfers between devices, local(): lax.psum_scatter(out_weight_grad, 'dp', scatter_dimension=1, tiled=True)  128 us
    while x80, local copies, waits for them, and re-layouts  50.8 us
    psum x1, blocking collectives, local(): lax.psum((gain_one_grad, shift_one_grad, out_bias_grad, gain_two_grad, sh...  42.1 us
    reduce_sum x2, other arithmetic, back_row(): bias_grad = bias_grad + jnp.sum(score_grad.astype(jnp.float32), axis=0)  40.7 us
    dot_general x4, matrix products, row_scores(): jnp.einsum('sqhd,khd->shqk', queries, keys_low, preferred_element_type=jn...  35.7 us
  transfers between devices with their start and end apart: 13, of which 12 were waited for; matrix products, arithmetic and copies ran while one was open for 7% of the time, Pallas kernels for 0%

commit v1 on v0

v1 whole, which is shorter than its diff:
```python
import functools

import jax
import jax.numpy as jnp
import numpy as np
from jax import lax
from jax.experimental import pallas as pl
from jax.experimental.pallas import tpu as pltpu
from jax.sharding import PartitionSpec as P

norm_eps = 1e-05
big_negative = -1e30
root_half = 0.7071067811865476
root_two_pi_inv = 0.3989422804014327

tile = 128
reach = 2
span = (2 * reach + 1) * tile
wide = span + tile
NT = (((1,), (1,)), ((), ()))
NN = (((1,), (0,)), ((), ()))


def dot_f32(left, right, dims=NN):
    return lax.dot_general(left, right, dims, preferred_element_type=jnp.float32)


def bucket_of(offset):
    distance = np.abs(offset)
    limits = 8.0 * 2.0 ** (np.arange(1, 8) / 2.0)
    counted = (distance[..., None] >= limits).sum(axis=-1)
    bucket = np.where(distance < 8, distance, 8 + counted)
    return (np.minimum(bucket, 15) + 16 * (offset < 0)).astype(np.int32)


def band_one_hot(buckets):
    place = np.arange(wide)
    offset = np.where(place < span, place, place - wide) - reach * tile
    return (bucket_of(offset)[:, None] == np.arange(buckets)[None, :]).astype(np.float32)


def key_tiles(b, tiles):
    return list(range(max(0, b - reach), min(tiles - 1, b + reach) + 1))


def attend_kernel(info_ref, t_ref, q_ref, k_ref, v_ref, o_ref, e_ref, linv_ref, mask_ref):
    row_len = k_ref.shape[0]
    tiles = row_len // tile

    @pl.when(pl.program_id(0) == 0)
    def _():
        seg = info_ref[0:1, :]
        order = info_ref[1:2, :]
        flag = info_ref[2:3, :]
        at = lax.broadcasted_iota(jnp.int32, (1, row_len), 1)
        first = (seg != pltpu.roll(seg, 1, 1)) | (at == 0)
        key_content = jnp.where(flag == 0.0, -1.0, order)
        key_query = jnp.where(first, -1.0, key_content)

        def as_column(row):
            return jnp.transpose(jnp.broadcast_to(row, (tile, row_len)))

        seg_col, content_col, query_col = as_column(seg), as_column(key_content), as_column(key_query)
        for b in range(tiles):
            here = slice(b * tile, (b + 1) * tile)
            same = seg_col == seg[:, here]
            mask_ref[b, :, :tile] = jnp.where(same & (content_col <= order[:, here]), 0.0, big_negative)
            mask_ref[b, :, tile:] = jnp.where(same & (query_col < order[:, here]), 0.0, big_negative)

    lane = lax.broadcasted_iota(jnp.int32, (1, tile), 1)
    v_t = jnp.transpose(v_ref[...].astype(jnp.float32)).astype(jnp.bfloat16)
    keys = k_ref[...].astype(jnp.float32) * 0.125
    half = tile // 2
    parts = [[None, None] for _ in range(tiles)]
    for h in range(2):
        in_head = (lane >= h * half) & (lane < (h + 1) * half)
        k_head = jnp.where(in_head, keys, 0.0).astype(jnp.bfloat16)
        band = pltpu.roll(jnp.broadcast_to(t_ref[h], (tile, wide)), 0, 1, stride=1, stride_axis=0)
        for b in range(tiles):
            near = key_tiles(b, tiles)
            q_tile = jnp.concatenate(
                [q_ref[b * tile : (b + 1) * tile, :], q_ref[row_len + b * tile : row_len + (b + 1) * tile, :]], axis=0
            )
            scores = []
            top = None
            for kb in near:
                d = b - kb + reach
                bias = band[:, d * tile : (d + 1) * tile]
                s = dot_f32(k_head[kb * tile : (kb + 1) * tile, :], q_tile, NT)
                s = s + jnp.concatenate([bias, bias], axis=1) + mask_ref[b, kb * tile : (kb + 1) * tile, :]
                scores.append(s)
                one_top = jnp.max(s, axis=0, keepdims=True)
                top = one_top if top is None else jnp.maximum(top, one_top)
            total = None
            weights = []
            for kb, s in zip(near, scores):
                e = jnp.exp(s - top)
                one_total = jnp.sum(e, axis=0, keepdims=True)
                total = one_total if total is None else total + one_total
                e = e.astype(jnp.bfloat16)
                e_ref[0, h, b, kb * tile : (kb + 1) * tile, :] = e
                weights.append(e)
            inverse = 1.0 / total
            linv_ref[0, h * tiles + b : h * tiles + b + 1, :] = inverse
            mixed = dot_f32(
                v_t[h * half : (h + 1) * half, near[0] * tile : (near[-1] + 1) * tile],
                jnp.concatenate(weights, axis=0),
            )
            parts[b][h] = mixed * inverse
    for b in range(tiles):
        both = jnp.transpose(jnp.concatenate(parts[b], axis=0)).astype(jnp.bfloat16)
        o_ref[b * tile : (b + 1) * tile, :] = both[:tile]
        o_ref[row_len + b * tile : row_len + (b + 1) * tile, :] = both[tile:]


def attend(info, band_rows, q, k, v):
    tokens, width = q.shape
    row_len = k.shape[0]
    pairs = width // tile
    tiles = row_len // tile
    pair_block = lambda rows: pl.BlockSpec((rows, tile), lambda p: (0, p))
    return pl.pallas_call(
        attend_kernel,
        grid=(pairs,),
        in_specs=[
            pl.BlockSpec(info.shape, lambda p: (0, 0)),
            pl.BlockSpec((2, 1, wide), lambda p: (p, 0, 0)),
            pair_block(tokens),
            pair_block(row_len),
            pair_block(row_len),
        ],
        out_specs=[
            pair_block(tokens),
            pl.BlockSpec((1, 2, tiles, row_len, 2 * tile), lambda p: (p, 0, 0, 0, 0)),
            pl.BlockSpec((1, 2 * tiles, 2 * tile), lambda p: (p, 0, 0)),
        ],
        out_shape=[
            jax.ShapeDtypeStruct((tokens, width), jnp.bfloat16),
            jax.ShapeDtypeStruct((pairs, 2, tiles, row_len, 2 * tile), jnp.bfloat16),
            jax.ShapeDtypeStruct((pairs, 2 * tiles, 2 * tile), jnp.float32),
        ],
        scratch_shapes=[pltpu.VMEM((tiles, row_len, 2 * tile), jnp.float32)],
        compiler_params=pltpu.CompilerParams(vmem_limit_bytes=40 * 1024 * 1024),
        cost_estimate=pl.CostEstimate(
            flops=pairs * 2 * 2 * 2 * 2 * row_len * row_len * 128,
            bytes_accessed=pairs * 2 * tiles * row_len * 2 * tile * 2,
            transcendentals=pairs * 4 * row_len * row_len,
        ),
        name="attend",
    )(info, band_rows, q, k, v)


def attend_back_kernel(q_ref, k_ref, v_ref, do_ref, o_ref, e_ref, linv_ref, dq_ref, dk_ref, dv_ref, band_ref, dk_acc, dv_acc, g_acc):
    row_len = k_ref.shape[0]
    tiles = row_len // tile
    half = tile // 2
    lane = lax.broadcasted_iota(jnp.int32, (1, tile), 1)
    k_t = jnp.transpose(k_ref[...].astype(jnp.float32)).astype(jnp.bfloat16)
    dk_acc[...] = jnp.zeros_like(dk_acc)
    dv_acc[...] = jnp.zeros_like(dv_acc)
    g_acc[...] = jnp.zeros_like(g_acc)
    for b in range(tiles):
        near = key_tiles(b, tiles)
        keys = slice(near[0] * tile, (near[-1] + 1) * tile)
        here = slice(b * tile, (b + 1) * tile)
        there = slice(row_len + b * tile, row_len + (b + 1) * tile)
        q_tile = jnp.concatenate([q_ref[here, :], q_ref[there, :]], axis=0)
        do_t = jnp.transpose(jnp.concatenate([do_ref[here, :], do_ref[there, :]], axis=0).astype(jnp.float32))
        o_t = jnp.transpose(jnp.concatenate([o_ref[here, :], o_ref[there, :]], axis=0).astype(jnp.float32))
        prod = do_t * o_t
        e_heads, ds_heads, do_heads, q_heads, dq_heads = [], [], [], [], []
        for h in range(2):
            mine = slice(h * half, (h + 1) * half)
            inverse = linv_ref[0, h * tiles + b : h * tiles + b + 1, :]
            delta = jnp.sum(prod[mine], axis=0, keepdims=True) * inverse
            scaled = do_t[mine] * inverse
            blank = jnp.zeros_like(scaled)
            do_head = jnp.concatenate([scaled, blank] if h == 0 else [blank, scaled], axis=0).astype(jnp.bfloat16)
            e_all, ds_all = [], []
            for kb in near:
                d = b - kb + reach
                rows = slice(kb * tile, (kb + 1) * tile)
                e = e_ref[0, h, b, rows, :]
                dp = dot_f32(v_ref[rows, :], do_head)
                ds = e.astype(jnp.float32) * (dp - delta)
                g_acc[h, :, d * tile : (d + 1) * tile] += ds[:, :tile] + ds[:, tile:]
                e_all.append(e)
                ds_all.append(ds.astype(jnp.bfloat16))
            ds_all = jnp.concatenate(ds_all, axis=0)
            e_heads.append(jnp.concatenate(e_all, axis=0))
            ds_heads.append(ds_all)
            do_heads.append(do_head)
            in_head = (lane >= h * half) & (lane < (h + 1) * half)
            q_heads.append(jnp.where(in_head, q_tile.astype(jnp.float32), 0.0).astype(jnp.bfloat16))
            dq_heads.append(dot_f32(k_t[mine, keys], ds_all))
        dv_acc[keys, :] += dot_f32(jnp.concatenate(e_heads, axis=1), jnp.concatenate(do_heads, axis=1), NT)
        dk_acc[keys, :] += dot_f32(jnp.concatenate(ds_heads, axis=1), jnp.concatenate(q_heads, axis=0))
        dq = (jnp.transpose(jnp.concatenate(dq_heads, axis=0)) * 0.125).astype(jnp.bfloat16)
        dq_ref[here, :] = dq[:tile]
        dq_ref[there, :] = dq[tile:]
    dk_ref[...] = (dk_acc[...] * 0.125).astype(jnp.bfloat16)
    dv_ref[...] = dv_acc[...].astype(jnp.bfloat16)
    row = lax.broadcasted_iota(jnp.int32, (8, wide), 0)
    for h in range(2):
        fold = g_acc[h, tile - 8 : tile, :]
        for a in range(tile // 8 - 2, -1, -1):
            fold = g_acc[h, 8 * a : 8 * a + 8, :] + pltpu.roll(fold, wide - 8, 1)
        for bit in (1, 2, 4):
            fold = jnp.where((row & bit) != 0, pltpu.roll(fold, wide - bit, 1), fold)
        band_ref[h] = jnp.sum(fold, axis=0, keepdims=True)


def attend_back(q, k, v, do, o, e, linv):
    tokens, width = q.shape
    row_len = k.shape[0]
    pairs = width // tile
    tiles = row_len // tile
    pair_block = lambda rows: pl.BlockSpec((rows, tile), lambda p: (0, p))
    return pl.pallas_call(
        attend_back_kernel,
        grid=(pairs,),
        in_specs=[
            pair_block(tokens),
            pair_block(row_len),
            pair_block(row_len),
            pair_block(tokens),
            pair_block(tokens),
            pl.BlockSpec((1, 2, tiles, row_len, 2 * tile), lambda p: (p, 0, 0, 0, 0)),
            pl.BlockSpec((1, 2 * tiles, 2 * tile), lambda p: (p, 0, 0)),
        ],
        out_specs=[
            pair_block(tokens),
            pair_block(row_len),
            pair_block(row_len),
            pl.BlockSpec((2, 1, wide), lambda p: (p, 0, 0)),
        ],
        out_shape=[
            jax.ShapeDtypeStruct((tokens, width), jnp.bfloat16),
            jax.ShapeDtypeStruct((row_len, width), jnp.bfloat16),
            jax.ShapeDtypeStruct((row_len, width), jnp.bfloat16),
            jax.ShapeDtypeStruct((2 * pairs, 1, wide), jnp.float32),
        ],
        scratch_shapes=[
            pltpu.VMEM((row_len, tile), jnp.float32),
            pltpu.VMEM((row_len, tile), jnp.float32),
            pltpu.VMEM((2, tile, wide), jnp.float32),
        ],
        compiler_params=pltpu.CompilerParams(vmem_limit_bytes=40 * 1024 * 1024),
        cost_estimate=pl.CostEstimate(
            flops=pairs * 2 * 2 * 4 * 2 * row_len * row_len * 128,
            bytes_accessed=pairs * 2 * tiles * row_len * 2 * tile * 2,
            transcendentals=0,
        ),
        name="attend_back",
    )(q, k, v, do, o, e, linv)


def layer_norm(values, gain_vec, shift_vec):
    centre = jnp.mean(values, axis=-1, keepdims=True)
    centred = values - centre
    variance = jnp.mean(centred * centred, axis=-1, keepdims=True)
    inv_scale = lax.rsqrt(variance + norm_eps)
    normed = centred * inv_scale
    return (normed * gain_vec + shift_vec, normed, inv_scale)


def norm_back(upstream, normed, inv_scale, gain_vec):
    scaled = upstream * gain_vec
    centre = jnp.mean(scaled, axis=-1, keepdims=True)
    along_normed = jnp.mean(scaled * normed, axis=-1, keepdims=True)
    return inv_scale * (scaled - centre - normed * along_normed)


def gelu_parts(pre_act):
    normal_cdf = 0.5 * (1.0 + lax.erf(pre_act * root_half))
    slope = normal_cdf + pre_act * jnp.exp(-0.5 * pre_act * pre_act) * root_two_pi_inv
    return (pre_act * normal_cdf, slope)


def exchange(value, axis_name, bit):
    count = lax.axis_size(axis_name)
    return lax.ppermute(value, axis_name, [(i, i ^ bit) for i in range(count)])


def scatter_sum(own_part, order):
    count = lax.axis_size("dp")
    index = lax.axis_index("dp")
    rows, n = own_part.shape
    block = rows // count
    left = list(range(count.bit_length() - 2, -1, -1))
    value = own_part
    for bit in order:
        at = left.index(bit)
        split = value.reshape(2**at, 2, 2 ** (len(left) - at - 1), block, n)
        mine = (index >> bit) & 1
        sent = lax.dynamic_index_in_dim(split, 1 - mine, 1, keepdims=False).astype(jnp.bfloat16)
        kept = lax.dynamic_index_in_dim(split, mine, 1, keepdims=False)
        value = kept.astype(jnp.float32) + exchange(sent, "dp", 1 << bit).astype(jnp.float32)
        left.remove(bit)
    return value.reshape(block, n)


def sum_all(vector):
    for bit in [1 << b for b in range(lax.axis_size("dp").bit_length() - 1)]:
        vector = vector + exchange(vector, "dp", bit)
    return vector + exchange(vector, "tensor", 1)


def local(
    content_input,
    query_input,
    segment_ids,
    orders,
    predicted,
    query_weight,
    query_bias,
    key_weight,
    value_weight,
    value_bias,
    out_weight,
    out_bias,
    first_gain,
    first_shift,
    up_weight,
    up_bias,
    down_weight,
    down_bias,
    second_gain,
    second_shift,
    bias_table,
    content_upstream,
    query_upstream,
):
    tensor_index = lax.axis_index("tensor")
    row_len = segment_ids.shape[1]
    bits = lax.axis_size("dp").bit_length() - 1
    ways = (
        list(range(bits)),
        [1, 0] + list(range(2, bits)),
        list(range(2, bits)) + [0, 1],
    )

    def cross(value):
        return exchange(value, "tensor", 1)

    def half_of(first, second):
        return jnp.where(tensor_index == 0, first, second)

    query_w = (query_weight, cross(query_weight))
    key_w = (key_weight, cross(key_weight))
    value_w = (value_weight, cross(value_weight))
    query_b = (query_bias, cross(query_bias))
    value_b = (value_bias, cross(value_bias))
    table = jnp.concatenate([bias_table, cross(bias_table)], axis=1)
    out_w = (out_weight, cross(out_weight))
    up_w = (up_weight, cross(up_weight))
    up_b = (up_bias, cross(up_bias))
    down_w = (down_weight, cross(down_weight))

    def own_rows(value):
        return lax.dynamic_slice_in_dim(value, tensor_index * row_len, row_len, 0)

    content = own_rows(content_input)
    streams = jnp.concatenate([content, own_rows(query_input)], axis=0)
    one_row = lambda value: lax.dynamic_index_in_dim(value, tensor_index, 0, keepdims=False)
    info = jnp.stack([one_row(segment_ids), one_row(orders), one_row(predicted)]).astype(jnp.float32)
    info = jnp.concatenate([info, jnp.zeros((5, row_len), jnp.float32)], axis=0)

    heads = bias_table.shape[1]
    one_hot = jnp.asarray(band_one_hot(bias_table.shape[0]))
    band_rows = jnp.einsum("mb,bh->hm", one_hot, table, precision=lax.Precision.HIGHEST)[:, None, :]

    saved = []
    for s in range(2):
        q = (dot_f32(streams, query_w[s]) + query_b[s]).astype(jnp.bfloat16)
        k = dot_f32(content, key_w[s]).astype(jnp.bfloat16)
        v = (dot_f32(content, value_w[s]) + value_b[s]).astype(jnp.bfloat16)
        o, e, linv = attend(info, band_rows[s * heads : (s + 1) * heads], q, k, v)
        saved.append((q, k, v, o, e, linv))
    mixed = [saved[0][3], saved[1][3]]
    attn = dot_f32(mixed[0], out_w[0]) + dot_f32(mixed[1], out_w[1])
    first, first_normed, first_inv = layer_norm(
        streams.astype(jnp.float32) + attn + out_bias, first_gain, first_shift
    )
    first_low = first.astype(jnp.bfloat16)
    hidden, slope = [], []
    for s in range(2):
        act, grad = gelu_parts(dot_f32(first_low, up_w[s]) + up_b[s])
        hidden.append(act.astype(jnp.bfloat16))
        slope.append(grad.astype(jnp.bfloat16))
    down = dot_f32(hidden[0], down_w[0]) + dot_f32(hidden[1], down_w[1])
    final, second_normed, second_inv = layer_norm(first + down + down_bias, second_gain, second_shift)
    final_low = final.astype(jnp.bfloat16)

    upstream = jnp.concatenate([content_upstream, query_upstream], axis=0).astype(jnp.float32)
    second_grad = norm_back(upstream, second_normed, second_inv, second_gain)
    gain_two_grad = jnp.sum(upstream * second_normed, axis=0)
    shift_two_grad = jnp.sum(upstream, axis=0)
    down_bias_grad = jnp.sum(second_grad, axis=0)
    down_low = second_grad.astype(jnp.bfloat16)

    TN = (((0,), (0,)), ((), ()))

    def pair_sum(make, order):
        far = cross(make(1).astype(jnp.bfloat16))
        return scatter_sum(make(0) + far.astype(jnp.float32), order)

    down_weight_grad = pair_sum(lambda s: dot_f32(down_low, hidden[s], TN), ways[0])
    up_low = [(dot_f32(down_low, down_w[s], NT) * slope[s].astype(jnp.float32)).astype(jnp.bfloat16) for s in range(2)]
    up_weight_grad = pair_sum(lambda s: dot_f32(first_low, up_low[s], TN), ways[1])
    up_bias_grad = [jnp.sum(up_low[s].astype(jnp.float32), axis=0) for s in range(2)]
    first_back = second_grad + dot_f32(up_low[0], up_w[0], NT) + dot_f32(up_low[1], up_w[1], NT)
    residual = norm_back(first_back, first_normed, first_inv, first_gain)
    gain_one_grad = jnp.sum(first_back * first_normed, axis=0)
    shift_one_grad = jnp.sum(first_back, axis=0)
    out_bias_grad = jnp.sum(residual, axis=0)
    attn_low = residual.astype(jnp.bfloat16)
    out_weight_grad = pair_sum(lambda s: dot_f32(attn_low, mixed[s], TN), ways[2])

    grads = [None, None]
    for s in (1, 0):
        q, k, v, o, e, linv = saved[s]
        mixed_grad = dot_f32(attn_low, out_w[s], NT).astype(jnp.bfloat16)
        grads[s] = attend_back(q, k, v, mixed_grad, o, e, linv)
    query_weight_grad = pair_sum(lambda s: dot_f32(streams, grads[s][0], TN), ways[0])
    key_weight_grad = pair_sum(lambda s: dot_f32(content, grads[s][1], TN), ways[1])
    value_weight_grad = pair_sum(lambda s: dot_f32(content, grads[s][2], TN), ways[2])
    query_bias_grad = [jnp.sum(grads[s][0].astype(jnp.float32), axis=0) for s in range(2)]
    value_bias_grad = [jnp.sum(grads[s][2].astype(jnp.float32), axis=0) for s in range(2)]
    band_grads = jnp.concatenate([grads[s][3][:, 0, :] for s in range(2)], axis=0)
    table_grad = jnp.einsum("mb,hm->hb", one_hot, band_grads, precision=lax.Precision.HIGHEST)
    from_query = dot_f32(grads[0][0], query_w[0], NT) + dot_f32(grads[1][0], query_w[1], NT) + residual
    content_grad = from_query[:row_len]
    for s in range(2):
        content_grad = content_grad + dot_f32(grads[s][1], key_w[s], NT) + dot_f32(grads[s][2], value_w[s], NT)
    query_grad = from_query[row_len:]

    def in_order(pair):
        return jnp.concatenate([half_of(pair[0], pair[1]), half_of(pair[1], pair[0])], axis=0)

    pieces = [
        gain_one_grad,
        shift_one_grad,
        out_bias_grad,
        gain_two_grad,
        shift_two_grad,
        down_bias_grad,
        in_order(query_bias_grad),
        in_order(value_bias_grad),
        in_order(up_bias_grad),
        in_order([table_grad[:heads], table_grad[heads:]]).reshape(-1),
    ]
    summed = sum_all(jnp.concatenate(pieces))
    ends = np.cumsum([0] + [piece.shape[0] for piece in pieces])
    out = [summed[ends[i] : ends[i + 1]] for i in range(len(pieces))]
    return (
        final_low[:row_len],
        final_low[row_len:],
        content_grad,
        query_grad,
        query_weight_grad,
        key_weight_grad,
        value_weight_grad,
        out_weight_grad.T,
        up_weight_grad,
        down_weight_grad.T,
        out[6],
        out[7],
        out[2],
        out[0],
        out[1],
        out[8],
        out[5],
        out[3],
        out[4],
        out[9].reshape(2 * heads, -1).T,
    )


def solution(mesh):
    placed = (
        P("dp", None),
        P("dp", None),
        P("dp", None),
        P("dp", None),
        P("dp", None),
        P(None, "tensor"),
        P("tensor"),
        P(None, "tensor"),
        P(None, "tensor"),
        P("tensor"),
        P("tensor", None),
        P(),
        P(),
        P(),
        P(None, "tensor"),
        P("tensor"),
        P("tensor", None),
        P(),
        P(),
        P(),
        P(None, "tensor"),
        P(("dp", "tensor"), None),
        P(("dp", "tensor"), None),
    )
    rows_out = P(("dp", "tensor"), None)
    return jax.shard_map(
        local,
        mesh=mesh,
        in_specs=placed,
        out_specs=(
            rows_out,
            rows_out,
            rows_out,
            rows_out,
            P("dp", "tensor"),
            P("dp", "tensor"),
            P("dp", "tensor"),
            P("tensor", "dp"),
            P("dp", "tensor"),
            P("tensor", "dp"),
        )
        + (P(),) * 10,
        check_vma=False,
    )
```

time: 1280 us -> 334 us (0.26)
  waiting for transfers between devices: 765 us -> 64.7 us
  local copies, waits for them, and re-layouts: 141 us -> 27.4 us
  matrix products: 203 us -> 125 us
  other arithmetic: 90.2 us -> 14.2 us
  Pallas kernels: 0 us -> 47.1 us
  starting transfers between devices: 1.12 us -> 48 us
  blocking collectives: 42.1 us -> 0 us
    reduce_scatter x8 -> x0, waiting for transfers between devices: 469 us -> none  [the longest x1 142 us: local(): lax.psum_scatter(up_weight_grad, 'dp', scatter_dimension=0, tiled=True)]
    unnamed x15 -> x0, waiting for transfers between devices: 256 us -> none
    dot_general x34 -> x38, matrix products: 203 us -> 125 us  [the longest x36 124 us: dot_f32(): lax.dot_general(left, right, dims, preferred_element_type=jnp.float32)]
    ppermute x0 -> x45, waiting for transfers between devices: none -> 64.7 us  [exchange(): return lax.ppermute(value, axis_name, [(i, i ^ bit) for i in range(count)])]
    reduce_sum x11 -> x7, other arithmetic: 69.6 us -> 5.54 us  [the longest x1 3.08 us: local(): down_bias_grad = jnp.sum(second_grad, axis=0)]
    while x84 -> x0, local copies, waits for them, and re-layouts: 62.5 us -> none
    ppermute x0 -> x45, starting transfers between devices: none -> 48 us  [exchange(): return lax.ppermute(value, axis_name, [(i, i ^ bit) for i in range(count)])]
    pallas_call x0 -> x4, Pallas kernels: none -> 47.1 us  [the longest x2 27 us: attend_back(): pl.pallas_call(attend_back_kernel, grid=(pairs,), in_specs=[pair_block(to...]
  transfers between devices with their start and end apart: 13 -> 45, of which waited for: 12 -> 19; matrix products, arithmetic and copies ran while one was open for 7% -> 31% of each run, Pallas kernels for 0% -> 6%
where the time goes in v1:
time: 334 us; the launch traced here: 329 us
  matrix products  125 us (37%)
  waiting for transfers between devices  64.7 us (19%)
  starting transfers between devices  48 us (14%)
  Pallas kernels  47.1 us (14%)
  local copies, waits for them, and re-layouts  27.4 us (8%)
  other arithmetic  14.2 us (4%)
    dot_general x36, matrix products, dot_f32(): lax.dot_general(left, right, dims, preferred_element_type=jnp.float32)  124 us
    ppermute x45, waiting for transfers between devices, exchange(): return lax.ppermute(value, axis_name, [(i, i ^ bit) for i in range(count)])  64.7 us
    ppermute x45, starting transfers between devices, exchange(): return lax.ppermute(value, axis_name, [(i, i ^ bit) for i in range(count)])  48 us
    pallas_call x2, Pallas kernels, attend_back(): pl.pallas_call(attend_back_kernel, grid=(pairs,), in_specs=[pair_block(to...  27 us
    unnamed x134, local copies, waits for them, and re-layouts  21 us
    pallas_call x2, Pallas kernels, attend(): pl.pallas_call(attend_kernel, grid=(pairs,), in_specs=[pl.BlockSpec(info....  20.1 us
  transfers between devices with their start and end apart: 45, of which 19 were waited for; matrix products, arithmetic and copies ran while one was open for 31% of the time, Pallas kernels for 6%

profile of v1, /device:TPU:0, one launch (start us, length us, event | category | flops | bytes accessed | tf_op | source)
XLA Modules:
  0.0 329.3 jit_solution(3448428225451717179)
XLA Ops:
  6.0 2.3 copy.91
  11.2 2.3 add_convert_fusion.2.q_ref
  13.6 2.6 copy.90
  17.8 10.2 %attend.2 = (bf16[1024,384]{1,0:T(8,128)(2,1)S(1)}, bf16[3,2,4,512,256]{4,3,2,1,0:T(8,128)(2,1)S(1)}, f32[3,8,256]{2,1,0:T(8,128)S(1)}) custom-call(f32[8,512]{1,0:T(8,128)S(1)} %concatenate.22.info_ref, f32[6,1,768]{2,1,0:T(1,128)S(1)} %slice.71.t_ref, bf16[1024,384]{1,0:T(8,128)(2,1)S(1)} %add_convert_fusion.2.q_ref, ...), custom_call_target="tpu_custom_call" | custom-call | flops 1610612736 | bytes 6291456 | tf_op jit(solution)/shard_map/attend/pallas_call | solution.py:122
  28.0 2.6 fusion.51
  35.2 2.1 add_convert_fusion.1.q_ref
  37.3 10.0 %attend.3 = (bf16[1024,384]{1,0:T(8,128)(2,1)S(1)}, bf16[3,2,4,512,256]{4,3,2,1,0:T(8,128)(2,1)S(1)}, f32[3,8,256]{2,1,0:T(8,128)S(1)}) custom-call(f32[8,512]{1,0:T(8,128)S(1)} %concatenate.22.info_ref, f32[6,1,768]{2,1,0:T(1,128)S(1)} %slice.73.t_ref, bf16[1024,384]{1,0:T(8,128)(2,1)S(1)} %add_convert_fusion.1.q_ref, ...), custom_call_target="tpu_custom_call" | custom-call | flops 1610612736 | bytes 6291456 | tf_op jit(solution)/shard_map/attend/pallas_call | solution.py:122
  47.3 3.6 %fusion.49 = (f32[1024]{0:T(1024)S(1)}, f32[1024,768]{0,1:T(8,128)S(1)}) fusion(f32[768]{0:T(1024)S(1)} %copy-done.45, f32[1024,768]{0,1:T(8,128)} %fusion.51, bf16[1024,384]{1,0:T(8,128)(2,1)S(1)} %get-tuple-element.35.o_ref, bf16[384,768]{1,0:T(8,128)(2,1)S(1)} %collective-permute-done.6, bf16[512,768]{0,1:T(8,128)(2,1)S(1)} %copy-done.21, ...), kind=kOutput, calls=%fused_computation.189 | convolution fusion | flops 610270208 | bytes 9247744 | tf_op jit(solution)/shard_map/dot_general | solution.py:25
  52.2 7.7 %multiply_convert_fusion.3 = (bf16[1024,1536]{1,0:T(8,128)(2,1)S(1)}, f32[1024,1536]{1,0:T(8,128)}) fusion(f32[1536]{0:T(1024)S(1)} %copy-done.49, bf16[1024,768]{0,1:T(8,128)(2,1)S(1)} %fusion.17, bf16[768,1536]{1,0:T(8,128)(2,1)} %param.38), kind=kOutput, calls=%fused_computation.18 | convolution fusion | flops 2425356288 | bytes 13375488 | tf_op jit(solution)/shard_map/dot_general | solution.py:25
  59.9 7.2 %fusion.52 = f32[1024,768]{0,1:T(8,128)} fusion(bf16[1024,1536]{1,0:T(8,128)(2,1)S(1)} %get-tuple-element.139, bf16[1536,768]{1,0:T(8,128)(2,1)} %param.40), kind=kOutput, calls=%fused_computation.192 | convolution fusion | flops 2415919104 | bytes 8650752 | tf_op jit(solution)/shard_map/dot_general | solution.py:25
  67.1 7.6 %multiply_convert_fusion.2 = (bf16[1024,1536]{1,0:T(8,128)(2,1)}, f32[1024,1536]{1,0:T(8,128)}) fusion(f32[1536]{0:T(1024)S(1)} %collective-permute-done.8, bf16[1024,768]{0,1:T(8,128)(2,1)S(1)} %fusion.17, bf16[768,1536]{1,0:T(8,128)(2,1)} %collective-permute-done.7), kind=kOutput, calls=%fused_computation.16 | convolution fusion | flops 2425356288 | bytes 13375488 | tf_op jit(solution)/shard_map/dot_general | solution.py:25
  74.7 7.1 %fusion.50 = (f32[1024]{0:T(1024)S(1)}, f32[1024,768]{0,1:T(8,128)S(1)}) fusion(f32[768]{0:T(1024)S(1)} %copy-done.50, f32[1024,768]{0,1:T(8,128)} %fusion.52, bf16[1024,1536]{1,0:T(8,128)(2,1)} %get-tuple-element.141, bf16[1536,768]{1,0:T(8,128)(2,1)} %collective-permute-done.9, f32[768]{0:T(1024)S(1)} %copy-done.46, f32[768]{0:T(1024)S(1)} %copy-done.42, ...), kind=kOutput, calls=%fused_computation.190 | convolution fusion | flops 2422209536 | bytes 14963712 | tf_op jit(solution)/shard_map/dot_general | solution.py:25
  84.1 3.1 fusion.42
  87.1 3.9 %convolution_convert_fusion = bf16[768,1536]{1,0:T(8,128)(2,1)} fusion(bf16[1024,768]{0,1:T(8,128)(2,1)S(1)} %get-tuple-element.119, bf16[1024,1536]{1,0:T(8,128)(2,1)S(1)} %copy-done.57), kind=kOutput, calls=%fused_computation.28 | convolution fusion | flops 2417098752 | bytes 7077888 | tf_op jit(solution)/shard_map/dot_general | solution.py:25
  91.1 7.2 %convert_reduce_fusion.1 = (f32[1536]{0:T(1024)S(1)}, bf16[1024,1536]{1,0:T(8,128)(2,1)S(1)}) fusion(f32[1024,1536]{1,0:T(8,128)} %get-tuple-element.140, f32[1536]{0:T(1024)S(1)} %copy-done.49, bf16[1024,768]{0,1:T(8,128)(2,1)S(1)} %get-tuple-element.119, bf16[1536,768]{1,0:T(8,128)(2,1)} %param.40), kind=kOutput, calls=%fused_computation.13 | convolution fusion | flops 2439510528 | bytes 13381632 | tf_op jit(solution)/shard_map/dot_general | solution.py:25
  98.3 7.1 %fusion.53 = f32[1024,768]{0,1:T(8,128)} fusion(bf16[1024,1536]{1,0:T(8,128)(2,1)S(1)} %get-tuple-element.147, bf16[768,1536]{1,0:T(8,128)(2,1)} %param.38), kind=kOutput, calls=%fused_computation.193 | convolution fusion | flops 2415919104 | bytes 8650752 | tf_op jit(solution)/shard_map/dot_general | solution.py:25
  105.4 7.2 %convert_reduce_fusion = (f32[1536]{0:T(1024)S(1)}, bf16[1024,1536]{1,0:T(8,128)(2,1)S(1)}) fusion(f32[1024,1536]{1,0:T(8,128)} %get-tuple-element.142, f32[1536]{0:T(1024)S(1)} %collective-permute-done.8, bf16[1024,768]{0,1:T(8,128)(2,1)S(1)} %get-tuple-element.119, bf16[1536,768]{1,0:T(8,128)(2,1)} %collective-permute-done.9), kind=kOutput, calls=%fused_computation.12 | convolution fusion | flops 2439510528 | bytes 13381632 | tf_op jit(solution)/shard_map/dot_general | solution.py:25
  114.3 3.8 %convolution_convert_fusion.1 = bf16[768,1536]{1,0:T(8,128)(2,1)} fusion(bf16[1024,768]{0,1:T(8,128)(2,1)S(1)} %copy-done.27, bf16[1024,1536]{1,0:T(8,128)(2,1)S(1)} %get-tuple-element.149), kind=kOutput, calls=%fused_computation.29 | convolution fusion | flops 2417098752 | bytes 7077888 | tf_op jit(solution)/shard_map/dot_general | solution.py:25
  118.2 8.0 %multiply_reduce_fusion = (f32[768]{0:T(1024)S(1)}, f32[1024]{0:T(1024)S(1)}, f32[1024]{0:T(1024)S(1)}, f32[768]{0:T(1024)S(1)}, f32[1024,768]{0,1:T(8,128)S(1)}) fusion(f32[1024,768]{0,1:T(8,128)S(1)} %get-tuple-element.138, f32[1024]{0:T(1024)S(1)} %add_rsqrt_fusion.1, f32[1024]{0:T(1024)S(1)} %broadcast_multiply_fusion.5, f32[768]{0:T(1024)S(1)} %copy-done.42, ...), kind=kOutput, calls=%fused_computation.34 | convolution fusion | flops 2433217024 | bytes 19705856 | tf_op jit(solution)/shard_map/dot_general | solution.py:25
  129.3 13.4 %attend_back.2 = (bf16[1024,384]{1,0:T(8,128)(2,1)S(1)}, bf16[512,384]{1,0:T(8,128)(2,1)S(1)}, bf16[512,384]{1,0:T(8,128)(2,1)S(1)}, f32[6,1,768]{2,1,0:T(1,128)S(1)}) custom-call(bf16[1024,384]{1,0:T(8,128)(2,1)S(1)} %copy-done.7, bf16[512,384]{1,0:T(8,128)(2,1)S(1)} %convolution_convert_fusion.9.k_ref, bf16[512,384]{1,0:T(8,128)(2,1)S(1)} %fusion.21.v_ref, ...), custom_call_target="tpu_custom_call" | custom-call | flops 3221225472 | bytes 6291456 | tf_op jit(solution)/shard_map/attend_back/pallas_call | solution.py:219
  142.8 2.7 fusion.54
  150.3 13.5 %attend_back.3 = (bf16[1024,384]{1,0:T(8,128)(2,1)S(1)}, bf16[512,384]{1,0:T(8,128)(2,1)S(1)}, bf16[512,384]{1,0:T(8,128)(2,1)S(1)}, f32[6,1,768]{2,1,0:T(1,128)S(1)}) custom-call(bf16[1024,384]{1,0:T(8,128)(2,1)S(1)} %add_convert_fusion.1.q_ref, bf16[512,384]{1,0:T(8,128)(2,1)S(1)} %convolution_convert_fusion.8.k_ref, bf16[512,384]{1,0:T(8,128)(2,1)S(1)} %fusion.22.v_ref, ...), custom_call_target="tpu_custom_call" | custom-call | flops 3221225472 | bytes 6291456 | tf_op jit(solution)/shard_map/attend_back/pallas_call | solution.py:219
  166.7 2.9 collective-permute-start.40
  169.6 4.1 %add_add_fusion = f32[1024,768]{0,1:T(8,128)S(1)} fusion(f32[1024,768]{0,1:T(8,128)} %copy-done.8, f32[1024,768]{0,1:T(8,128)} %fusion.54, bf16[1024,384]{1,0:T(8,128)(2,1)S(1)} %get-tuple-element.41, bf16[768,384]{1,0:T(8,128)(2,1)} %collective-permute-done.1), kind=kOutput, calls=%fused_computation.35 | convolution fusion | flops 605552640 | bytes 10813440 | tf_op jit(solution)/shard_map/dot_general | solution.py:25
  175.6 3.6 %fusion.45 = (f32[512,768]{0,1:T(8,128)}, f32[512,768]{0,1:T(8,128)}) fusion(f32[1024,768]{0,1:T(8,128)S(1)} %add_add_fusion, f32[512,768]{0,1:T(8,128)S(1)} %fusion.57, f32[512,768]{0,1:T(8,128)S(1)} %copy-done.15, f32[512,768]{0,1:T(8,128)S(1)} %copy-done.16, bf16[512,384]{1,0:T(8,128)(2,1)S(1)} %get-tuple-element.45, ...), kind=kOutput, calls=%fused_computation.185 | convolution fusion | flops 303562752 | bytes 11993088 | tf_op jit(solution)/shard_map/dot_general | solution.py:25
  189.3 2.6 collective-permute-start.43
  196.2 2.3 copy.108
  199.6 3.0 copy.110
  202.7 3.0 copy.111
  210.0 2.5 convert_add_fusion.6
  219.9 2.0 convert_add_fusion.3
  225.4 2.9 collective-permute-done.21
  229.8 3.3 collective-permute-done.26
  233.1 2.8 collective-permute-start.22
  238.0 8.2 %collective-permute-done.22 = bf16[1,4,48,384]{3,2,1,0:T(8,128)(2,1)S(1)} collective-permute-done((bf16[1,4,48,384]{3,2,1,0:T(8,128)(2,1)S(1)}, bf16[1,4,48,384]{3,2,1,0:T(8,128)(2,1)S(1)}, u32[]{:S(2)}, u32[]{:S(2)}) %collective-permute-start.22) | collective-permute-done | bytes 147488 | tf_op jit(solution)/shard_map/ppermute | solution.py:282
  246.3 2.0 collective-permute-done.27
  258.3 4.4 %convert_add_fusion.1 = f32[768,1536]{1,0:T(8,128)S(1)} fusion(bf16[768,1536]{1,0:T(8,128)(2,1)} %collective-permute-done.30, bf16[1024,768]{0,1:T(8,128)(2,1)S(1)} %copy-done.28, bf16[1024,1536]{1,0:T(8,128)(2,1)S(1)} %copy-done.56), kind=kOutput, calls=%fused_computation.24 | convolution fusion | flops 2418278400 | bytes 11796480 | tf_op jit(solution)/shard_map/dot_general | solution.py:25
  263.8 2.6 convert_add_fusion
  269.1 19.4 %collective-permute-done.31 = bf16[4,2,48,1536]{3,2,0,1:T(8,128)(2,1)S(1)} collective-permute-done((bf16[4,2,48,1536]{3,2,0,1:T(8,128)(2,1)S(1)}, bf16[4,2,48,1536]{3,2,0,1:T(8,128)(2,1)S(1)}, u32[]{:S(2)}, u32[]{:S(2)}) %collective-permute-start.31) | collective-permute-done | bytes 1179680 | tf_op jit(solution)/shard_map/ppermute | solution.py:282
  290.2 4.4 %collective-permute-done.36 = bf16[8,1,48,1536]{3,2,0,1:T(8,128)(2,1)S(1)} collective-permute-done((bf16[8,1,48,1536]{3,2,0,1:T(8,128)(2,1)S(1)}, bf16[8,1,48,1536]{3,2,0,1:T(8,128)(2,1)S(1)}, u32[]{:S(2)}, u32[]{:S(2)}) %collective-permute-start.36) | collective-permute-done | bytes 1179680 | tf_op jit(solution)/shard_map/ppermute | solution.py:282
  295.1 2.1 collective-permute-start.37
  297.2 7.0 %collective-permute-done.32 = bf16[4,1,48,1536]{3,2,0,1:T(8,128)(2,1)S(1)} collective-permute-done((bf16[4,1,48,1536]{3,2,0,1:T(8,128)(2,1)S(1)}, bf16[4,1,48,1536]{3,2,0,1:T(8,128)(2,1)S(1)}, u32[]{:S(2)}, u32[]{:S(2)}) %collective-permute-start.32) | collective-permute-done | bytes 589856 | tf_op jit(solution)/shard_map/ppermute | solution.py:282
  304.4 2.6 collective-permute-start.33
  308.4 7.1 %collective-permute-done.33 = bf16[2,1,48,1536]{3,2,0,1:T(8,128)(2,1)S(1)} collective-permute-done((bf16[2,1,48,1536]{3,2,0,1:T(8,128)(2,1)S(1)}, bf16[2,1,48,1536]{3,2,0,1:T(8,128)(2,1)S(1)}, u32[]{:S(2)}, u32[]{:S(2)}) %collective-permute-start.33) | collective-permute-done | bytes 294944 | tf_op jit(solution)/shard_map/ppermute | solution.py:282
  315.6 2.3 collective-permute-start.34
  319.1 3.8 %collective-permute-start.39 = (bf16[1,1,48,1536]{3,2,0,1:T(8,128)(2,1)S(1)}, bf16[1,1,48,1536]{3,2,0,1:T(8,128)(2,1)S(1)}, u32[]{:S(2)}, u32[]{:S(2)}) collective-permute-start(bf16[1,1,48,1536]{3,2,0,1:T(8,128)(2,1)S(1)} %dynamic-slice_convert_fusion.4), channel_id=1, source_target_pairs={{0,16},{2,18},{4,20},{6,22},{8,24},{10,26},{12,28},{14,30},{16,0},... | collective-permute-start | bytes 442376 | tf_op jit(solution)/shard_map/ppermute | solution.py:282
  322.8 2.1 collective-permute-done.34
  325.7 2.4 collective-permute-done.39
  (314 shorter events, 86.1 us)
Async XLA Ops:
  0.7 15.5 %collective-permute-start = (f32[32,6]{0,1:T(8,128)}, f32[32,6]{0,1:T(8,128)S(1)}, u32[]{:S(2)}, u32[]{:S(2)}) collective-permute-start(f32[32,6]{0,1:T(8,128)} %param.44), channel_id=1, source_target_pairs={{0,1},{1,0},{2,3},{3,2},{4,5},{5,4},{6,7},{7,6},{8,9},{9,8},{10,11... | collective-permute-start | bytes 2312 | tf_op jit(solution)/shard_map/ppermute | solution.py:282
  1.2 34.0 %collective-permute-start.1 = (bf16[768,384]{1,0:T(8,128)(2,1)}, bf16[768,384]{1,0:T(8,128)(2,1)}, u32[]{:S(2)}, u32[]{:S(2)}) collective-permute-start(bf16[768,384]{1,0:T(8,128)(2,1)} %param.29), channel_id=1, source_target_pairs={{0,1},{1,0},{2,3},{3,2},{4,5},{5,4},{6,7},{7,6},{8,9},{9,8},{10,11... | collective-permute-start | bytes 1769480 | tf_op jit(solution)/shard_map/ppermute | solution.py:282
  1.3 33.7 %collective-permute-start.2 = (f32[384]{0:T(512)}, f32[384]{0:T(512)S(1)}, u32[]{:S(2)}, u32[]{:S(2)}) collective-permute-start(f32[384]{0:T(512)} %param.30), channel_id=1, source_target_pairs={{0,1},{1,0},{2,3},{3,2},{4,5},{5,4},{6,7},{7,6},{8,9},{9,8},{10,11... | collective-permute-start | bytes 4616 | tf_op jit(solution)/shard_map/ppermute | solution.py:282
  1.7 31.2 %collective-permute-start.3 = (bf16[768,384]{1,0:T(8,128)(2,1)}, bf16[768,384]{1,0:T(8,128)(2,1)}, u32[]{:S(2)}, u32[]{:S(2)}) collective-permute-start(bf16[768,384]{1,0:T(8,128)(2,1)} %param.31), channel_id=1, source_target_pairs={{0,1},{1,0},{2,3},{3,2},{4,5},{5,4},{6,7},{7,6},{8,9},{9,8},{10,11... | collective-permute-start | bytes 1769480 | tf_op jit(solution)/shard_map/ppermute | solution.py:282
  1.8 29.4 %collective-permute-start.4 = (bf16[768,384]{1,0:T(8,128)(2,1)}, bf16[768,384]{1,0:T(8,128)(2,1)}, u32[]{:S(2)}, u32[]{:S(2)}) collective-permute-start(bf16[768,384]{1,0:T(8,128)(2,1)} %param.32), channel_id=1, source_target_pairs={{0,1},{1,0},{2,3},{3,2},{4,5},{5,4},{6,7},{7,6},{8,9},{9,8},{10,11... | collective-permute-start | bytes 1769480 | tf_op jit(solution)/shard_map/ppermute | solution.py:282
  3.7 29.7 %copy-start.9 = (bf16[512,768]{1,0:T(8,128)(2,1)}, bf16[512,768]{1,0:T(8,128)(2,1)S(1)}, u32[]{:S(2)}) copy-start(bf16[512,768]{1,0:T(8,128)(2,1)S(1)} %get-tuple-element.153) | copy-start | bytes 2359300
  16.1 14.5 %collective-permute-start.5 = (f32[384]{0:T(512)S(1)}, f32[384]{0:T(512)S(1)}, u32[]{:S(2)}, u32[]{:S(2)}) collective-permute-start(f32[384]{0:T(512)S(1)} %copy-done.51), channel_id=1, source_target_pairs={{0,1},{1,0},{2,3},{3,2},{4,5},{5,4},{6,7},{7,6},{8,9},{9,8},{10,11... | collective-permute-start | bytes 4616 | tf_op jit(solution)/shard_map/ppermute | solution.py:282
  30.6 16.6 %collective-permute-start.6 = (bf16[384,768]{1,0:T(8,128)(2,1)S(1)}, bf16[384,768]{1,0:T(8,128)(2,1)S(1)}, u32[]{:S(2)}, u32[]{:S(2)}) collective-permute-start(bf16[384,768]{1,0:T(8,128)(2,1)S(1)} %copy-done.32), channel_id=1, source_target_pairs={{0,1},{1,0},{2,3},{3,2},{4,5},{5,4},{6,7},{7,6},{8,9},{9,8},{10,11... | collective-permute-start | bytes 1769480 | tf_op jit(solution)/shard_map/ppermute | solution.py:282
  31.1 36.0 %collective-permute-start.8 = (f32[1536]{0:T(1024)S(1)}, f32[1536]{0:T(1024)S(1)}, u32[]{:S(2)}, u32[]{:S(2)}) collective-permute-start(f32[1536]{0:T(1024)S(1)} %copy-done.49), channel_id=1, source_target_pairs={{0,1},{1,0},{2,3},{3,2},{4,5},{5,4},{6,7},{7,6},{8,9},{9,8},{10,11... | collective-permute-start | bytes 18440 | tf_op jit(solution)/shard_map/ppermute | solution.py:282
  32.9 34.2 %collective-permute-start.7 = (bf16[768,1536]{1,0:T(8,128)(2,1)}, bf16[768,1536]{1,0:T(8,128)(2,1)}, u32[]{:S(2)}, u32[]{:S(2)}) collective-permute-start(bf16[768,1536]{1,0:T(8,128)(2,1)} %param.38), channel_id=1, source_target_pairs={{0,1},{1,0},{2,3},{3,2},{4,5},{5,4},{6,7},{7,6},{8,9},{9,8},{10,11... | collective-permute-start | bytes 7077896 | tf_op jit(solution)/shard_map/ppermute | solution.py:282
  35.0 39.7 %collective-permute-start.9 = (bf16[1536,768]{1,0:T(8,128)(2,1)}, bf16[1536,768]{1,0:T(8,128)(2,1)}, u32[]{:S(2)}, u32[]{:S(2)}) collective-permute-start(bf16[1536,768]{1,0:T(8,128)(2,1)} %param.40), channel_id=1, source_target_pairs={{0,1},{1,0},{2,3},{3,2},{4,5},{5,4},{6,7},{7,6},{8,9},{9,8},{10,11... | collective-permute-start | bytes 7077896 | tf_op jit(solution)/shard_map/ppermute | solution.py:282
  47.3 103.1 %copy-start.2 = (bf16[1024,384]{1,0:T(8,128)(2,1)}, bf16[1024,384]{1,0:T(8,128)(2,1)S(1)}, u32[]{:S(2)}) copy-start(bf16[1024,384]{1,0:T(8,128)(2,1)S(1)} %get-tuple-element.35.o_ref) | copy-start | bytes 2359300
  166.7 14.4 %collective-permute-start.40 = (f32[9600]{0:T(1024)}, f32[9600]{0:T(1024)S(1)}, u32[]{:S(2)}, u32[]{:S(2)}) collective-permute-start(f32[9600]{0:T(1024)} %constant_dynamic-update-slice_fusion), channel_id=1, source_target_pairs={{0,2},{2,0},{4,6},{6,4},{8,10},{10,8},{12,14},{14,12},{16,18},{18,... | collective-permute-start | bytes 115208 | tf_op jit(solution)/shard_map/ppermute | solution.py:282
  181.2 4.1 %collective-permute-start.41 = (f32[9600]{0:T(1024)S(1)}, f32[9600]{0:T(1024)S(1)}, u32[]{:S(2)}, u32[]{:S(2)}) collective-permute-start(f32[9600]{0:T(1024)S(1)} %add.419), channel_id=1, source_target_pairs={{0,4},{2,6},{4,0},{6,2},{8,12},{10,14},{12,8},{14,10},{16,20},{18,... | collective-permute-start | bytes 115208 | tf_op jit(solution)/shard_map/ppermute | solution.py:282
  185.2 4.0 %collective-permute-start.42 = (f32[9600]{0:T(1024)S(1)}, f32[9600]{0:T(1024)S(1)}, u32[]{:S(2)}, u32[]{:S(2)}) collective-permute-start(f32[9600]{0:T(1024)S(1)} %add.420), channel_id=1, source_target_pairs={{0,8},{2,10},{4,12},{6,14},{8,0},{10,2},{12,4},{14,6},{16,24},{18,... | collective-permute-start | bytes 115208 | tf_op jit(solution)/shard_map/ppermute | solution.py:282
  188.6 20.8 %collective-permute-start.10 = (bf16[768,384]{1,0:T(8,128)(2,1)}, bf16[768,384]{1,0:T(8,128)(2,1)}, u32[]{:S(2)}, u32[]{:S(2)}) collective-permute-start(bf16[768,384]{1,0:T(8,128)(2,1)} %convolution_convert_fusion.5), channel_id=1, source_target_pairs={{0,1},{1,0},{2,3},{3,2},{4,5},{5,4},{6,7},{7,6},{8,9},{9,8},{10,11... | collective-permute-start | bytes 1769480 | tf_op jit(solution)/shard_map/ppermute | solution.py:282
  189.3 4.9 %collective-permute-start.43 = (f32[9600]{0:T(1024)S(1)}, f32[9600]{0:T(1024)S(1)}, u32[]{:S(2)}, u32[]{:S(2)}) collective-permute-start(f32[9600]{0:T(1024)S(1)} %add.421), channel_id=1, source_target_pairs={{0,16},{2,18},{4,20},{6,22},{8,24},{10,26},{12,28},{14,30},{16,0},... | collective-permute-start | bytes 115208 | tf_op jit(solution)/shard_map/ppermute | solution.py:282
  194.8 11.9 %collective-permute-start.44 = (f32[9600]{0:T(1024)}, f32[9600]{0:T(1024)}, u32[]{:S(2)}, u32[]{:S(2)}) collective-permute-start(f32[9600]{0:T(1024)} %add.422), channel_id=1, source_target_pairs={{0,1},{1,0},{2,3},{3,2},{4,5},{5,4},{6,7},{7,6},{8,9},{9,8},{10,11... | collective-permute-start | bytes 115208 | tf_op jit(solution)/shard_map/ppermute | solution.py:282
  205.7 6.9 %collective-permute-start.15 = (bf16[768,384]{1,0:T(8,128)(2,1)}, bf16[768,384]{1,0:T(8,128)(2,1)}, u32[]{:S(2)}, u32[]{:S(2)}) collective-permute-start(bf16[768,384]{1,0:T(8,128)(2,1)} %convolution_convert_fusion.7), channel_id=1, source_target_pairs={{0,1},{1,0},{2,3},{3,2},{4,5},{5,4},{6,7},{7,6},{8,9},{9,8},{10,11... | collective-permute-start | bytes 1769480 | tf_op jit(solution)/shard_map/ppermute | solution.py:282
  206.2 8.6 %collective-permute-start.20 = (bf16[768,384]{1,0:T(8,128)(2,1)}, bf16[768,384]{1,0:T(8,128)(2,1)}, u32[]{:S(2)}, u32[]{:S(2)}) collective-permute-start(bf16[768,384]{1,0:T(8,128)(2,1)} %convolution_convert_fusion.6), channel_id=1, source_target_pairs={{0,1},{1,0},{2,3},{3,2},{4,5},{5,4},{6,7},{7,6},{8,9},{9,8},{10,11... | collective-permute-start | bytes 1769480 | tf_op jit(solution)/shard_map/ppermute | solution.py:282
  206.2 12.0 %collective-permute-start.25 = (bf16[768,384]{1,0:T(8,128)(2,1)}, bf16[768,384]{1,0:T(8,128)(2,1)}, u32[]{:S(2)}, u32[]{:S(2)}) collective-permute-start(bf16[768,384]{1,0:T(8,128)(2,1)} %convolution_convert_fusion.4), channel_id=1, source_target_pairs={{0,1},{1,0},{2,3},{3,2},{4,5},{5,4},{6,7},{7,6},{8,9},{9,8},{10,11... | collective-permute-start | bytes 1769480 | tf_op jit(solution)/shard_map/ppermute | solution.py:282
  206.7 51.5 %collective-permute-start.30 = (bf16[768,1536]{1,0:T(8,128)(2,1)}, bf16[768,1536]{1,0:T(8,128)(2,1)}, u32[]{:S(2)}, u32[]{:S(2)}) collective-permute-start(bf16[768,1536]{1,0:T(8,128)(2,1)} %convolution_convert_fusion.1), channel_id=1, source_target_pairs={{0,1},{1,0},{2,3},{3,2},{4,5},{5,4},{6,7},{7,6},{8,9},{9,8},{10,11... | collective-permute-start | bytes 7077896 | tf_op jit(solution)/shard_map/ppermute | solution.py:282
  209.4 54.4 %collective-permute-start.35 = (bf16[768,1536]{1,0:T(8,128)(2,1)}, bf16[768,1536]{1,0:T(8,128)(2,1)S(1)}, u32[]{:S(2)}, u32[]{:S(2)}) collective-permute-start(bf16[768,1536]{1,0:T(8,128)(2,1)} %convolution_convert_fusion), channel_id=1, source_target_pairs={{0,1},{1,0},{2,3},{3,2},{4,5},{5,4},{6,7},{7,6},{8,9},{9,8},{10,11... | collective-permute-start | bytes 7077896 | tf_op jit(solution)/shard_map/ppermute | solution.py:282
  212.6 9.4 %collective-permute-start.11 = (bf16[8,1,48,384]{3,2,0,1:T(8,128)(2,1)S(1)}, bf16[8,1,48,384]{3,2,0,1:T(8,128)(2,1)S(1)}, u32[]{:S(2)}, u32[]{:S(2)}) collective-permute-start(bf16[8,1,48,384]{3,2,0,1:T(8,128)(2,1)S(1)} %fusion.29), channel_id=1, source_target_pairs={{0,2},{2,0},{4,6},{6,4},{8,10},{10,8},{12,14},{14,12},{16,18},{18,... | collective-permute-start | bytes 884744 | tf_op jit(solution)/shard_map/ppermute | solution.py:282
  214.8 8.8 %collective-permute-start.16 = (bf16[4,2,48,384]{3,2,0,1:T(8,128)(2,1)S(1)}, bf16[4,2,48,384]{3,2,0,1:T(8,128)(2,1)S(1)}, u32[]{:S(2)}, u32[]{:S(2)}) collective-permute-start(bf16[4,2,48,384]{3,2,0,1:T(8,128)(2,1)S(1)} %fusion.28), channel_id=1, source_target_pairs={{0,4},{2,6},{4,0},{6,2},{8,12},{10,14},{12,8},{14,10},{16,20},{18,... | collective-permute-start | bytes 884744 | tf_op jit(solution)/shard_map/ppermute | solution.py:282
  218.3 10.0 %collective-permute-start.21 = (bf16[2,4,48,384]{3,2,1,0:T(8,128)(2,1)S(1)}, bf16[2,4,48,384]{3,2,1,0:T(8,128)(2,1)S(1)}, u32[]{:S(2)}, u32[]{:S(2)}) collective-permute-start(bf16[2,4,48,384]{3,2,1,0:T(8,128)(2,1)S(1)} %fusion.30), channel_id=1, source_target_pairs={{0,8},{2,10},{4,12},{6,14},{8,0},{10,2},{12,4},{14,6},{16,24},{18,... | collective-permute-start | bytes 884744 | tf_op jit(solution)/shard_map/ppermute | solution.py:282
  222.0 11.1 %collective-permute-start.26 = (bf16[2,4,48,384]{3,2,1,0:T(8,128)(2,1)S(1)}, bf16[2,4,48,384]{3,2,1,0:T(8,128)(2,1)S(1)}, u32[]{:S(2)}, u32[]{:S(2)}) collective-permute-start(bf16[2,4,48,384]{3,2,1,0:T(8,128)(2,1)S(1)} %fusion.31), channel_id=1, source_target_pairs={{0,8},{2,10},{4,12},{6,14},{8,0},{10,2},{12,4},{14,6},{16,24},{18,... | collective-permute-start | bytes 884744 | tf_op jit(solution)/shard_map/ppermute | solution.py:282
  223.6 12.5 %collective-permute-start.12 = (bf16[4,1,48,384]{3,2,0,1:T(8,128)(2,1)S(1)}, bf16[4,1,48,384]{3,2,0,1:T(8,128)(2,1)S(1)}, u32[]{:S(2)}, u32[]{:S(2)}) collective-permute-start(bf16[4,1,48,384]{3,2,0,1:T(8,128)(2,1)S(1)} %fusion.32), channel_id=1, source_target_pairs={{0,4},{2,6},{4,0},{6,2},{8,12},{10,14},{12,8},{14,10},{16,20},{18,... | collective-permute-start | bytes 442376 | tf_op jit(solution)/shard_map/ppermute | solution.py:282
  228.2 8.1 %collective-permute-start.17 = (bf16[4,1,48,384]{3,2,0,1:T(8,128)(2,1)S(1)}, bf16[4,1,48,384]{3,2,0,1:T(8,128)(2,1)S(1)}, u32[]{:S(2)}, u32[]{:S(2)}) collective-permute-start(bf16[4,1,48,384]{3,2,0,1:T(8,128)(2,1)S(1)} %dynamic-slice_convert_fusion.8), channel_id=1, source_target_pairs={{0,2},{2,0},{4,6},{6,4},{8,10},{10,8},{12,14},{14,12},{16,18},{18,... | collective-permute-start | bytes 442376 | tf_op jit(solution)/shard_map/ppermute | solution.py:282
  233.1 13.1 %collective-permute-start.22 = (bf16[1,4,48,384]{3,2,1,0:T(8,128)(2,1)S(1)}, bf16[1,4,48,384]{3,2,1,0:T(8,128)(2,1)S(1)}, u32[]{:S(2)}, u32[]{:S(2)}) collective-permute-start(bf16[1,4,48,384]{3,2,1,0:T(8,128)(2,1)S(1)} %dynamic-slice_convert_fusion.7), channel_id=1, source_target_pairs={{0,16},{2,18},{4,20},{6,22},{8,24},{10,26},{12,28},{14,30},{16,0},... | collective-permute-start | bytes 442376 | tf_op jit(solution)/shard_map/ppermute | solution.py:282
  235.9 22.3 %copy-start.28 = (bf16[1024,768]{0,1:T(8,128)(2,1)S(1)}, bf16[1024,768]{0,1:T(8,128)(2,1)}, u32[]{:S(2)}) copy-start(bf16[1024,768]{0,1:T(8,128)(2,1)} %copy-done.26) | copy-start | bytes 4718596
  236.0 12.3 %collective-permute-start.27 = (bf16[1,4,48,384]{3,2,1,0:T(8,128)(2,1)S(1)}, bf16[1,4,48,384]{3,2,1,0:T(8,128)(2,1)S(1)}, u32[]{:S(2)}, u32[]{:S(2)}) collective-permute-start(bf16[1,4,48,384]{3,2,1,0:T(8,128)(2,1)S(1)} %dynamic-slice_convert_fusion.6), channel_id=1, source_target_pairs={{0,16},{2,18},{4,20},{6,22},{8,24},{10,26},{12,28},{14,30},{16,0},... | collective-permute-start | bytes 442376 | tf_op jit(solution)/shard_map/ppermute | solution.py:282
  236.3 13.3 %collective-permute-start.13 = (bf16[2,1,48,384]{3,2,0,1:T(8,128)(2,1)S(1)}, bf16[2,1,48,384]{3,2,0,1:T(8,128)(2,1)S(1)}, u32[]{:S(2)}, u32[]{:S(2)}) collective-permute-start(bf16[2,1,48,384]{3,2,0,1:T(8,128)(2,1)S(1)} %fusion.33), channel_id=1, source_target_pairs={{0,8},{2,10},{4,12},{6,14},{8,0},{10,2},{12,4},{14,6},{16,24},{18,... | collective-permute-start | bytes 221192 | tf_op jit(solution)/shard_map/ppermute | solution.py:282
  246.2 4.4 %collective-permute-start.18 = (bf16[2,1,48,384]{3,2,0,1:T(8,128)(2,1)S(1)}, bf16[2,1,48,384]{3,2,0,1:T(8,128)(2,1)S(1)}, u32[]{:S(2)}, u32[]{:S(2)}) collective-permute-start(bf16[2,1,48,384]{3,2,0,1:T(8,128)(2,1)S(1)} %fusion.34), channel_id=1, source_target_pairs={{0,8},{2,10},{4,12},{6,14},{8,0},{10,2},{12,4},{14,6},{16,24},{18,... | collective-permute-start | bytes 221192 | tf_op jit(solution)/shard_map/ppermute | solution.py:282
  248.3 4.4 %collective-permute-start.23 = (bf16[2,1,48,384]{3,2,0,1:T(8,128)(2,1)S(1)}, bf16[2,1,48,384]{3,2,0,1:T(8,128)(2,1)S(1)}, u32[]{:S(2)}, u32[]{:S(2)}) collective-permute-start(bf16[2,1,48,384]{3,2,0,1:T(8,128)(2,1)S(1)} %fusion.35), channel_id=1, source_target_pairs={{0,2},{2,0},{4,6},{6,4},{8,10},{10,8},{12,14},{14,12},{16,18},{18,... | collective-permute-start | bytes 221192 | tf_op jit(solution)/shard_map/ppermute | solution.py:282
  249.6 4.7 %collective-permute-start.28 = (bf16[2,1,48,384]{3,2,0,1:T(8,128)(2,1)S(1)}, bf16[2,1,48,384]{3,2,0,1:T(8,128)(2,1)S(1)}, u32[]{:S(2)}, u32[]{:S(2)}) collective-permute-start(bf16[2,1,48,384]{3,2,0,1:T(8,128)(2,1)S(1)} %fusion.36), channel_id=1, source_target_pairs={{0,2},{2,0},{4,6},{6,4},{8,10},{10,8},{12,14},{14,12},{16,18},{18,... | collective-permute-start | bytes 221192 | tf_op jit(solution)/shard_map/ppermute | solution.py:282
  250.6 4.9 %collective-permute-start.14 = (bf16[1,1,48,384]{3,2,0,1:T(8,128)(2,1)S(1)}, bf16[1,1,48,384]{3,2,0,1:T(8,128)(2,1)S(1)}, u32[]{:S(2)}, u32[]{:S(2)}) collective-permute-start(bf16[1,1,48,384]{3,2,0,1:T(8,128)(2,1)S(1)} %dynamic-slice_convert_fusion.17), channel_id=1, source_target_pairs={{0,16},{2,18},{4,20},{6,22},{8,24},{10,26},{12,28},{14,30},{16,0},... | collective-permute-start | bytes 110600 | tf_op jit(solution)/shard_map/ppermute | solution.py:282
  252.7 4.9 %collective-permute-start.19 = (bf16[1,1,48,384]{3,2,0,1:T(8,128)(2,1)S(1)}, bf16[1,1,48,384]{3,2,0,1:T(8,128)(2,1)S(1)}, u32[]{:S(2)}, u32[]{:S(2)}) collective-permute-start(bf16[1,1,48,384]{3,2,0,1:T(8,128)(2,1)S(1)} %dynamic-slice_convert_fusion.16), channel_id=1, source_target_pairs={{0,16},{2,18},{4,20},{6,22},{8,24},{10,26},{12,28},{14,30},{16,0},... | collective-permute-start | bytes 110600 | tf_op jit(solution)/shard_map/ppermute | solution.py:282
  254.3 13.5 %collective-permute-start.24 = (bf16[1,1,48,384]{3,2,0,1:T(8,128)(2,1)S(1)}, bf16[1,1,48,384]{3,2,0,1:T(8,128)(2,1)S(1)}, u32[]{:S(2)}, u32[]{:S(2)}) collective-permute-start(bf16[1,1,48,384]{3,2,0,1:T(8,128)(2,1)S(1)} %dynamic-slice_convert_fusion.15), channel_id=1, source_target_pairs={{0,4},{2,6},{4,0},{6,2},{8,12},{10,14},{12,8},{14,10},{16,20},{18,... | collective-permute-start | bytes 110600 | tf_op jit(solution)/shard_map/ppermute | solution.py:282
  255.5 13.0 %collective-permute-start.29 = (bf16[1,1,48,384]{3,2,0,1:T(8,128)(2,1)S(1)}, bf16[1,1,48,384]{3,2,0,1:T(8,128)(2,1)S(1)}, u32[]{:S(2)}, u32[]{:S(2)}) collective-permute-start(bf16[1,1,48,384]{3,2,0,1:T(8,128)(2,1)S(1)} %dynamic-slice_convert_fusion.14), channel_id=1, source_target_pairs={{0,4},{2,6},{4,0},{6,2},{8,12},{10,14},{12,8},{14,10},{16,20},{18,... | collective-permute-start | bytes 110600 | tf_op jit(solution)/shard_map/ppermute | solution.py:282
  262.9 25.6 %collective-permute-start.31 = (bf16[4,2,48,1536]{3,2,0,1:T(8,128)(2,1)S(1)}, bf16[4,2,48,1536]{3,2,0,1:T(8,128)(2,1)S(1)}, u32[]{:S(2)}, u32[]{:S(2)}) collective-permute-start(bf16[4,2,48,1536]{3,2,0,1:T(8,128)(2,1)S(1)} %fusion.23), channel_id=1, source_target_pairs={{0,4},{2,6},{4,0},{6,2},{8,12},{10,14},{12,8},{14,10},{16,20},{18,... | collective-permute-start | bytes 3538952 | tf_op jit(solution)/shard_map/ppermute | solution.py:282
  266.6 28.0 %collective-permute-start.36 = (bf16[8,1,48,1536]{3,2,0,1:T(8,128)(2,1)S(1)}, bf16[8,1,48,1536]{3,2,0,1:T(8,128)(2,1)S(1)}, u32[]{:S(2)}, u32[]{:S(2)}) collective-permute-start(bf16[8,1,48,1536]{3,2,0,1:T(8,128)(2,1)S(1)} %fusion.24), channel_id=1, source_target_pairs={{0,2},{2,0},{4,6},{6,4},{8,10},{10,8},{12,14},{14,12},{16,18},{18,... | collective-permute-start | bytes 3538952 | tf_op jit(solution)/shard_map/ppermute | solution.py:282
  289.0 15.2 %collective-permute-start.32 = (bf16[4,1,48,1536]{3,2,0,1:T(8,128)(2,1)S(1)}, bf16[4,1,48,1536]{3,2,0,1:T(8,128)(2,1)S(1)}, u32[]{:S(2)}, u32[]{:S(2)}) collective-permute-start(bf16[4,1,48,1536]{3,2,0,1:T(8,128)(2,1)S(1)} %dynamic-slice_convert_fusion.1), channel_id=1, source_target_pairs={{0,2},{2,0},{4,6},{6,4},{8,10},{10,8},{12,14},{14,12},{16,18},{18,... | collective-permute-start | bytes 1769480 | tf_op jit(solution)/shard_map/ppermute | solution.py:282
  295.1 11.9 %collective-permute-start.37 = (bf16[4,1,48,1536]{3,2,0,1:T(8,128)(2,1)S(1)}, bf16[4,1,48,1536]{3,2,0,1:T(8,128)(2,1)S(1)}, u32[]{:S(2)}, u32[]{:S(2)}) collective-permute-start(bf16[4,1,48,1536]{3,2,0,1:T(8,128)(2,1)S(1)} %fusion.25), channel_id=1, source_target_pairs={{0,4},{2,6},{4,0},{6,2},{8,12},{10,14},{12,8},{14,10},{16,20},{18,... | collective-permute-start | bytes 1769480 | tf_op jit(solution)/shard_map/ppermute | solution.py:282
  304.4 11.1 %collective-permute-start.33 = (bf16[2,1,48,1536]{3,2,0,1:T(8,128)(2,1)S(1)}, bf16[2,1,48,1536]{3,2,0,1:T(8,128)(2,1)S(1)}, u32[]{:S(2)}, u32[]{:S(2)}) collective-permute-start(bf16[2,1,48,1536]{3,2,0,1:T(8,128)(2,1)S(1)} %fusion.26), channel_id=1, source_target_pairs={{0,8},{2,10},{4,12},{6,14},{8,0},{10,2},{12,4},{14,6},{16,24},{18,... | collective-permute-start | bytes 884744 | tf_op jit(solution)/shard_map/ppermute | solution.py:282
  307.2 11.8 %collective-permute-start.38 = (bf16[2,1,48,1536]{3,2,0,1:T(8,128)(2,1)S(1)}, bf16[2,1,48,1536]{3,2,0,1:T(8,128)(2,1)S(1)}, u32[]{:S(2)}, u32[]{:S(2)}) collective-permute-start(bf16[2,1,48,1536]{3,2,0,1:T(8,128)(2,1)S(1)} %fusion.27), channel_id=1, source_target_pairs={{0,8},{2,10},{4,12},{6,14},{8,0},{10,2},{12,4},{14,6},{16,24},{18,... | collective-permute-start | bytes 884744 | tf_op jit(solution)/shard_map/ppermute | solution.py:282
  315.6 9.3 %collective-permute-start.34 = (bf16[1,1,48,1536]{3,2,0,1:T(8,128)(2,1)S(1)}, bf16[1,1,48,1536]{3,2,0,1:T(8,128)(2,1)S(1)}, u32[]{:S(2)}, u32[]{:S(2)}) collective-permute-start(bf16[1,1,48,1536]{3,2,0,1:T(8,128)(2,1)S(1)} %dynamic-slice_convert_fusion.5), channel_id=1, source_target_pairs={{0,16},{2,18},{4,20},{6,22},{8,24},{10,26},{12,28},{14,30},{16,0},... | collective-permute-start | bytes 442376 | tf_op jit(solution)/shard_map/ppermute | solution.py:282
  319.1 9.0 %collective-permute-start.39 = (bf16[1,1,48,1536]{3,2,0,1:T(8,128)(2,1)S(1)}, bf16[1,1,48,1536]{3,2,0,1:T(8,128)(2,1)S(1)}, u32[]{:S(2)}, u32[]{:S(2)}) collective-permute-start(bf16[1,1,48,1536]{3,2,0,1:T(8,128)(2,1)S(1)} %dynamic-slice_convert_fusion.4), channel_id=1, source_target_pairs={{0,16},{2,18},{4,20},{6,22},{8,24},{10,26},{12,28},{14,30},{16,0},... | collective-permute-start | bytes 442376 | tf_op jit(solution)/shard_map/ppermute | solution.py:282
  (56 other events, 375.6 us)
